TPU v7x, 128 devices: a whole 4x4x4 slice. The times are simulated.
128 devices in a mesh: dp: 8 (over z_hi, y), factor: 16 (over z_lo, x, core).
Axes of the slice: x: 4, y: 4, z: 4 (z_hi: 2, z_lo: 2; z = z_hi * 2 + z_lo), core: 2. Of those that a mesh axis runs over, the one named last changes fastest.
Arguments:
- features: bfloat16 [2048, 16, 2048], P('dp', 'factor'), may hold values from -135 to 135
- previous: float32 [16, 2048, 2048], P('factor'), may hold values from -40 to 40, as said below
- gradient: bfloat16 [16, 2, 2048, 2048], P('factor', None, 'dp'), may hold values from -6 to 6
Outputs:
- factor: float32 [16, 2048, 2048], P('factor', 'dp')
- preconditioned: bfloat16 [16, 2, 2048, 2048], P('factor', None, None, 'dp')
Inputs may be any that keep to these rules, and one draw needn't show every extreme that they name: `previous`: every block is symmetric and positive definite.
All inputs are finite; a program needn't handle non-finite values.
Results may differ from a plain program's by a relative error of at most 0.0049.
Values may be sent and summed in bfloat16 or wider, within the bound.
A program may use at most 320 MiB of HBM per device.

v0:
```python
import math

import jax
import jax.numpy as jnp
from jax import lax
from jax.sharding import PartitionSpec as P

decay_rate = 0.5
damping = 0.1
highest = lax.Precision.HIGHEST


def shifted(shard, axis, by):
    devices = lax.axis_size(axis)
    return lax.ppermute(shard, axis, [(i, (i + by) % devices) for i in range(devices)])


def tile_width(size_total):
    return 256 if size_total % 256 == 0 else size_total


def dot_high(left, right):
    return jnp.dot(left, right, precision=highest)


def dot_left_transposed(left, right):
    return lax.dot_general(left, right, (((0,), (0,)), ((), ())), precision=highest)


def blocked_cholesky(matrix, diag_shift):
    size_total = matrix.shape[0]
    width = tile_width(size_total)
    count = size_total // width
    eye_tile = jnp.eye(width, dtype=jnp.float32)
    trailing = matrix
    inverses = []
    panels = []
    columns = []
    for step in range(count):
        head = trailing[:width, :width] + diag_shift * eye_tile
        lower_tile = jnp.linalg.cholesky(head)
        inverse_tile = jax.scipy.linalg.solve_triangular(lower_tile, eye_tile, lower=True)
        inverses.append(inverse_tile)
        pieces = []
        if step > 0:
            pieces.append(jnp.zeros((step * width, width), jnp.float32))
        pieces.append(lower_tile)
        if step + 1 < count:
            below = trailing[width:, :width]
            panel = lax.dot_general(
                below, inverse_tile, (((1,), (1,)), ((), ())), precision=highest
            )
            panels.append(panel)
            pieces.append(panel)
            trailing = trailing[width:, width:] - lax.dot_general(
                panel, panel, (((1,), (1,)), ((), ())), precision=highest
            )
        columns.append(jnp.concatenate(pieces, axis=0))
    return (jnp.concatenate(columns, axis=1), (inverses, panels))


def split_factor(lower_factor):
    size_total = lower_factor.shape[0]
    width = tile_width(size_total)
    count = size_total // width
    eye_tile = jnp.eye(width, dtype=jnp.float32)
    inverses = []
    panels = []
    for step in range(count):
        start = step * width
        lower_tile = lower_factor[start : start + width, start : start + width]
        inverses.append(jax.scipy.linalg.solve_triangular(lower_tile, eye_tile, lower=True))
        if step + 1 < count:
            panels.append(lower_factor[start + width :, start : start + width])
    return (inverses, panels)


def solve_both(tiles, right_side):
    inverses, panels = tiles
    count = len(inverses)
    width = inverses[0].shape[0]
    remaining = right_side
    forward = []
    for step in range(count):
        head = dot_high(inverses[step], remaining[:width])
        forward.append(head)
        if step + 1 < count:
            remaining = remaining[width:] - dot_high(panels[step], head)
    later = None
    for step in reversed(range(count)):
        value = forward[step]
        if later is not None:
            value = value - dot_left_transposed(panels[step], later)
        solved = dot_left_transposed(inverses[step], value)
        later = solved if later is None else jnp.concatenate([solved, later], axis=0)
    return later


def per_device(features, previous, gradient):
    layers = lax.axis_size("factor") // 8
    factor_index = lax.axis_index("factor")
    layer_index = factor_index % layers
    member = factor_index // layers
    block_size = previous.shape[1]
    row_count = block_size // lax.axis_size("dp")
    total_tokens = features.shape[0] * lax.axis_size("dp")
    weight = (1.0 - decay_rate) / total_tokens
    own_tokens = features[:, 0, :]
    slot_ids = jnp.arange(2 * layers)
    slot_hot = jnp.where(slot_ids == 2 * layer_index + member % 2, 1.0, 0.0).astype(jnp.float32)
    summed = lax.psum_scatter(
        lax.dot_general(
            own_tokens, own_tokens, (((0,), (0,)), ((), ())), preferred_element_type=jnp.float32
        ),
        "dp",
        scatter_dimension=0,
        tiled=True,
    )
    stale_rows = lax.dynamic_slice_in_dim(
        previous[0], lax.axis_index("dp") * row_count, row_count, 0
    )
    own_rows = decay_rate * stale_rows + weight * summed
    factor = lax.all_gather(own_rows, "dp", axis=0, tiled=True)
    traces = lax.psum(jnp.trace(factor) * slot_hot, "factor")
    input_trace = jnp.sum(jnp.where(slot_ids == 2 * layer_index, traces, 0.0))
    grad_trace = jnp.sum(jnp.where(slot_ids == 2 * layer_index + 1, traces, 0.0))
    pi_ratio = jnp.sqrt(input_trace / grad_trace)
    diag_shift = jnp.where(member % 2 == 0, pi_ratio, 1.0 / pi_ratio) * math.sqrt(damping)
    lower_factor, own_tiles = blocked_cholesky(factor, diag_shift)
    tile_rows = gradient.shape[2]
    flattened = gradient[0].reshape(2 * tile_rows, block_size).astype(jnp.float32)
    section_one = solve_both(own_tiles, flattened.T).T.astype(jnp.bfloat16)
    section_one = section_one.reshape(1, 2, tile_rows, block_size)
    transposed = lax.all_to_all(section_one, "dp", split_axis=3, concat_axis=2, tiled=True)
    results = []
    for tile_index in range(2):
        partner = shifted(lower_factor, "factor", layers * (2 * tile_index + 1))
        finished = solve_both(split_factor(partner), transposed[0, tile_index].astype(jnp.float32))
        results.append(finished.astype(jnp.bfloat16))
    preconditioned = jnp.stack(results)[None]
    return (own_rows[None], preconditioned)


def solution(mesh):
    placed = (P("dp", "factor", None), P("factor", None, None), P("factor", None, "dp", None))
    return jax.shard_map(
        per_device,
        mesh=mesh,
        in_specs=placed,
        out_specs=(P("factor", "dp", None), P("factor", None, None, "dp")),
        check_vma=False,
    )
```

profile of v0, /device:TPU:0, one launch (start us, length us, event | category | flops | bytes accessed | tf_op | source)
XLA Modules:
  0.0 2426.1 jit_solution(8943356355912434559)
XLA Ops:
  21.7 190.6 %reduce-scatter.2.cloned.1.call-done = f32[256,2048]{0,1:T(8,128)} async-done(((f32[2048,2048]{0,1:T(8,128)}), f32[256,2048]{0,1:T(8,128)}) %reduce-scatter.2.cloned.1.call-update) | async-done | bytes 2097168 | tf_op jit(solution)/shard_map/reduce_scatter | solution.py:111
  216.8 204.8 %all-gather.2.cloned.1.call-done = f32[2048,2048]{0,1:T(8,128)} async-done(((f32[256,2048]{0,1:T(8,128)}), f32[2048,2048]{0,1:T(8,128)}) %all-gather.2.cloned.1.call-update) | async-done | bytes 16777232 | tf_op jit(solution)/shard_map/all_gather | solution.py:123
  429.5 28.6 %psum.7 = f32[4]{0:T(128)S(1)} all-reduce(f32[4]{0:T(128)S(1)} %fusion.345), channel_id=1, replica_groups=mesh['dp'=8,'factor'=16] {'factor'}, use_global_device_ids=true, to_apply=%region_2.3 | all-reduce | flops 4 | bytes 32 | tf_op jit(solution)/shard_map/psum | solution.py:124
  462.2 11.7 cholesky.382
  484.3 11.7 cholesky.399
  502.5 19.9 custom-call.42
  528.1 15.4 slice_subtract_fusion
  549.4 11.7 cholesky.416
  572.1 11.7 cholesky.433
  590.3 19.8 custom-call.44
  615.4 11.9 convolution_subtract_fusion.1
  632.2 11.7 cholesky.450
  654.9 11.7 cholesky.467
  673.7 20.1 custom-call.46
  710.6 11.7 cholesky.484
  733.3 11.7 cholesky.501
  751.4 19.9 custom-call.48
  785.0 11.7 cholesky.518
  807.7 11.7 cholesky.535
  826.4 19.9 custom-call.50
  856.8 11.7 cholesky.552
  881.2 12.1 cholesky.569
  901.4 19.7 custom-call.52
  933.0 13.2 cholesky.586
  948.4 11.3 custom-call.53
  964.7 13.3 cholesky.603
  992.0 21.1 custom-call.54
  1025.4 13.2 cholesky.620
  1040.5 11.3 custom-call.55
  1058.2 13.6 cholesky.637
  1107.3 21.1 custom-call.57
  1185.1 655.0 %all-to-all-done = bf16[1,2,256,2048]{2,1,0,3:T(2,128)(2,1)} async-done(((bf16[1,2,256,2048]{2,1,0,3:T(2,128)(2,1)}), bf16[1,2,256,2048]{2,1,0,3:T(2,128)(2,1)}, u32[]{:S(2)}, u32[]{:S(2)}) %all-to-all-start) | async-done | bytes 2097184 | tf_op jit(solution)/shard_map/all_to_all | solution.py:134
  1899.0 21.1 custom-call.65
  1921.3 21.1 custom-call.72
  1942.4 21.1 custom-call.71
  1963.5 21.1 custom-call.70
  1984.6 21.3 custom-call.69
  2005.8 21.1 custom-call.68
  2026.9 21.1 custom-call.67
  2048.1 21.3 custom-call.66
  2138.9 20.7 custom-call.64
  2165.6 21.1 custom-call.63
  2192.2 21.1 custom-call.62
  2219.2 21.1 custom-call.61
  2247.9 21.1 custom-call.60
  2276.7 21.5 custom-call.59
  2305.9 21.1 custom-call.58
  2334.3 21.2 custom-call.56
  (741 shorter events, 708.0 us)
Async XLA Ops:
  7.2 205.1 %reduce-scatter.2.cloned.1.call-start = ((), (), s32[]{:S(2)}) async-start(), calls=%async_computation.2 | async-start | bytes 18874368 | tf_op jit(solution)/shard_map/reduce_scatter | solution.py:111
  16.6 405.1 %all-gather.2.cloned.1.call-start = ((), (), s32[]{:S(2)}) async-start(), calls=%async_computation.3 | async-start | bytes 18874368 | tf_op jit(solution)/shard_map/all_gather | solution.py:123
  522.8 5.3 copy-start.31
  523.5 20.0 copy-start.45
  543.5 4.7 copy-start.2
  610.5 4.9 copy-start.33
  611.2 16.1 copy-start.47
  615.4 11.9 copy-start.3
  627.4 3.7 copy-start.5
  694.8 11.9 copy-start.35
  698.4 8.3 copy-start.6
  709.4 38.2 %copy-start.78 = (s32[2,2]{1,0:T(2,128)S(1)}, s32[2,2]{1,0:T(2,128)}, u32[]{:S(2)}) copy-start(s32[2,2]{1,0:T(2,128)} %copy-done.77) | copy-start | bytes 52
  771.7 10.2 copy-start.23
  772.4 9.4 copy-start.37
  775.5 6.4 copy-start.11
  826.4 20.6 copy-start.79
  846.6 7.6 copy-start.25
  847.3 6.9 copy-start.39
  849.9 297.7 %copy-start.9 = (f32[768,256]{1,0:T(8,128)}, f32[768,256]{1,0:T(8,128)S(1)}, u32[]{:S(2)}) copy-start(f32[768,256]{1,0:T(8,128)S(1)} %fusion.111) | copy-start | bytes 2359300
  856.8 12.4 copy-start.58
  1082.5 3.1 copy-start.7
  1082.5 3.1 copy-start.51
  1082.5 3.1 copy-start.75
  1095.7 749.1 %collective-permute-start.1 = (f32[2048,2048]{1,0:T(8,128)}, f32[2048,2048]{1,0:T(8,128)}, u32[]{:S(2)}, u32[]{:S(2)}) collective-permute-start(f32[2048,2048]{1,0:T(8,128)} %pad_dynamic-update-slice_fusion), channel_id=1, source_target_pairs={{0,6},{1,7},{2,8},{3,9},{4,10},{5,11},{6,12},{7,13},{8,14},{9,15},... | collective-permute-start | bytes 50331656 | tf_op jit(solution)/shard_map/ppermute | solution.py:15
  1095.7 4.6 copy-start.80
  1128.5 5.2 copy-start.21
  1133.6 3.4 copy-start.34
  1133.7 3.4 copy-start.48
  1133.7 4.0 copy-start.4
  1141.8 3.0 copy-start.13
  1169.2 3.3 copy-start.32
  1169.2 3.3 copy-start.46
  1175.9 5.2 copy-start.15
  1175.9 664.2 %all-to-all-start = ((bf16[1,2,256,2048]{2,1,0,3:T(2,128)(2,1)}), bf16[1,2,256,2048]{2,1,0,3:T(2,128)(2,1)}, u32[]{:S(2)}, u32[]{:S(2)}) async-start(bf16[1,2,256,2048]{2,1,0,3:T(2,128)(2,1)} %bitcast.695), calls=%async_computation.1 | async-start | bytes 4194304 | tf_op jit(solution)/shard_map/all_to_all | solution.py:134
  1182.9 948.6 %collective-permute-start = (f32[2048,2048]{1,0:T(8,128)}, f32[2048,2048]{1,0:T(8,128)}, u32[]{:S(2)}, u32[]{:S(2)}) collective-permute-start(f32[2048,2048]{1,0:T(8,128)} %pad_dynamic-update-slice_fusion), channel_id=1, source_target_pairs={{0,2},{1,3},{2,4},{3,5},{4,6},{5,7},{6,8},{7,9},{8,10},{9,11},{10,... | collective-permute-start | bytes 50331656 | tf_op jit(solution)/shard_map/ppermute | solution.py:15
  1851.3 26.5 %copy-start.71 = (f32[2,128,128]{2,1,0:T(8,128)}, f32[2,128,128]{2,1,0:T(8,128)S(1)}, u32[]{:S(2)}) copy-start(f32[2,128,128]{2,1,0:T(8,128)S(1)} %get-tuple-element.173) | copy-start | bytes 393220
  1891.1 7.9 copy-start.72
  2069.4 8.5 copy-start.70
  2069.4 8.8 copy-start.69
  2069.4 10.8 copy-start.68
  2073.0 8.2 copy-start.67
  2076.6 5.6 copy-start.66
  2078.5 4.7 copy-start.65
  2355.5 7.3 copy-start.64
  2355.5 9.2 copy-start.63
  2356.8 9.9 copy-start.62
  2360.4 7.3 copy-start.61
  2363.1 5.6 copy-start.60
  (38 other events, 58.7 us)
Sparse Core Ops, SparseCore 0:
  16.7 195.5 reduce-scatter.1
  215.6 205.9 all-gather.1
where the time goes:
time: 2440 us; the launch traced here: 2430 us
  waiting for transfers between devices  1050 us (43%)
  other arithmetic  843 us (35%)
  matrix products  265 us (11%)
  local copies, waits for them, and re-layouts  202 us (8%)
  between operations  29.3 us (1%)
  blocking collectives  28.6 us (1%)
    all_to_all x1, waiting for transfers between devices, per_device(): lax.all_to_all(section_one, 'dp', split_axis=3, concat_axis=2, tiled=True)  655 us
    another operation x18, other arithmetic, split_factor(): jax.scipy.linalg.solve_triangular(lower_tile, eye_tile, lower=True)  343 us
    another operation x55, other arithmetic, blocked_cholesky(): lower_tile = jnp.linalg.cholesky(head)  293 us
    all_gather x1, waiting for transfers between devices, per_device(): factor = lax.all_gather(own_rows, 'dp', axis=0, tiled=True)  205 us
    reduce_scatter x1, waiting for transfers between devices, per_device(): lax.psum_scatter(lax.dot_general(own_tokens, own_tokens, (((0,), (0,)), (...  191 us
    another operation x17, other arithmetic, blocked_cholesky(): jax.scipy.linalg.solve_triangular(lower_tile, eye_tile, lower=True)  169 us
    another operation x96, local copies, waits for them, and re-layouts, split_factor(): jax.scipy.linalg.solve_triangular(lower_tile, eye_tile, lower=True)  94.3 us
    dot_general x45, matrix products, dot_left_transposed(): lax.dot_general(left, right, (((0,), (0,)), ((), ())), precision=highest)  72.8 us
  transfers between devices with their start and end apart: 5, of which 3 were waited for; matrix products, arithmetic and copies ran while one was open for 16% of the time, Pallas kernels for 0%

commit v1 on v0

v1 whole, which is shorter than its diff:
```python
import math
import jax, jax.numpy as jnp, numpy as np, functools
from jax import lax
from jax.experimental import pallas as pl
from jax.experimental.pallas import tpu as pltpu
W=256

def inv2(a,b,c):
    r = 1.0/(a*c-b*b)
    return c*r, -b*r, a*r

def inv4(p):
    a,b,c = inv2(p[0][0],p[0][1],p[1][1])
    b00,b01,b10,b11 = p[0][2],p[0][3],p[1][2],p[1][3]
    w00=a*b00+b*b10; w01=a*b01+b*b11; w10=b*b00+c*b10; w11=b*b01+c*b11
    s00=p[2][2]-(b00*w00+b10*w10); s01=p[2][3]-(b00*w01+b10*w11); s11=p[3][3]-(b01*w01+b11*w11)
    d00,d01,d11=inv2(s00,s01,s11)
    x00=-(w00*d00+w01*d01); x01=-(w00*d01+w01*d11); x10=-(w10*d00+w11*d01); x11=-(w10*d01+w11*d11)
    t00=a-(x00*w00+x01*w01); t01=b-(x00*w10+x01*w11); t11=c-(x10*w10+x11*w11)
    return [[t00,t01,x00,x01],[t01,t11,x10,x11],[x00,x10,d00,d01],[x01,x11,d01,d11]]

def invq(p,q):
    if q==1: return [[1.0/p[0][0]]]
    if q==2:
        a,b,c=inv2(p[0][0],p[0][1],p[1][1]); return [[a,b],[b,c]]
    return inv4(p)

NN=(((1,),(0,)),((),())); NT=(((1,),(1,)),((),()))
bf=jnp.bfloat16; f32=jnp.float32
def split(x):
    hi=x.astype(bf); return hi,(x-hi.astype(f32)).astype(bf)
def dot3(a,b,dims):
    d=lambda x,y: lax.dot_general(x,y,dims,preferred_element_type=f32)
    return d(a[0],b[0])+(d(a[0],b[1])+d(a[1],b[0]))

def sweep(A, slot, q=4, n=128):
    lane = lax.broadcasted_iota(jnp.int32,(1,n),1)
    for s in range(0,n,q):
        rows=[A[s+i:s+i+1,:] for i in range(q)]
        p=[[jnp.broadcast_to(rows[i][:,s+j:s+j+1],(1,n)) if j>=i else None for j in range(q)] for i in range(q)]
        X=invq(p,q)
        inl=(lane>=s)&(lane<s+q)
        rm=[jnp.where(lane==s+i,1.0,jnp.where(inl,0.0,rows[i])) for i in range(q)]
        nr=[]
        for i in range(q):
            t=X[i][0]*rm[0]
            for j in range(1,q): t=t+X[i][j]*rm[j]
            nr.append(t)
        tiles=[]
        for r in range(0,n,8):
            T=A[r:r+8,:]
            cols=[jnp.broadcast_to(T[:,s+i:s+i+1],(8,n)) for i in range(q)]
            T=jnp.where(inl,0.0,T)
            if r<=s<r+8:
                ri=lax.broadcasted_iota(jnp.int32,(8,1),0)+r
                inr=(ri>=s)&(ri<s+q)
                T=jnp.where(inr,0.0,T)
                cols=[jnp.where(ri==s+i,-1.0,jnp.where(inr,0.0,cols[i])) for i in range(q)]
            for i in range(q): T=T-cols[i]*nr[i]
            tiles.append(T)
        A=jnp.concatenate(tiles,axis=0)
        slot(s//q)
    return A

def tables(nb, extra, slots):
    dst=np.zeros((nb,slots),np.int32); li=np.zeros((nb,slots),np.int32); rj=np.zeros((nb,slots),np.int32)
    dst[:]=nb-1
    for k in range(1,nb):
        t=0
        for j in range(k,nb):
            for i in range(j,nb+extra):
                if (i,j)==(k,k): continue
                dst[k,t]=i*nb+j; li[k,t]=i; rj[k,t]=j; t+=1
        assert t<=slots
    return dst,li,rj

def factor_kernel(nb, extra, interleave, dst_t, li_t, rj_t, a_hbm, g_hbm, chi_hbm, clo_hbm, phi_o, plo_o, s_o,
                  blk, chi, clo, uh, ul, ch, cl, half, asem, gsem, osem):
    nr=nb+extra
    copies=[]
    for j in range(nb):
        cs=[]
        for i in range(j,nb):
            cs.append(pltpu.make_async_copy(a_hbm.at[pl.ds(i*W,W),pl.ds(j*W,W)], blk.at[i*nb+j], asem.at[i,j]))
        for e in range(extra):
            cs.append(pltpu.make_async_copy(g_hbm.at[pl.ds(e*W,W),pl.ds(j*W,W)], blk.at[(nb+e)*nb+j], gsem.at[e,j]))
        for c in cs: c.start()
        copies+=cs
    for c in copies: c.wait()

    def tile(k,t):
        d=dst_t[k,t]; i=li_t[k,t]; j=rj_t[k,t]
        blk[d]=blk[d]-dot3((ch[i],cl[i]),(uh[j],ul[j]),NT)

    def step(k,_):
        kk=k*nb+k
        half[0]=blk[kk,:128,:128]
        def hbody(h,_):
            fn=(lambda s: tile(k,h*32+s)) if interleave else (lambda s:None)
            p=sweep(half[h],fn)
            half[h]=p
            @pl.when(h==0)
            def _():
                d21=split(blk[kk,128:,:128])
                w=dot3(d21,split(p),NN)
                half[2]=w
                half[1]=blk[kk,128:,128:]-dot3(split(w),d21,NT)
            return 0
        lax.fori_loop(0,2,hbody,0)
        p2=split(half[1]); w=half[2]
        x21=-dot3(p2,split(w),NN)
        wt=split(w.T)
        x11=half[0]-dot3(wt,split(x21),NN)
        x12=x21.T
        top=jnp.concatenate([x11,x12],axis=1)
        bot=jnp.concatenate([x21,half[1]],axis=1)
        P=split(jnp.concatenate([top,bot],axis=0))
        phi_o[k]=P[0]; plo_o[k]=P[1]
        if not interleave:
            def lp(t,_):
                tile(k,t); return 0
            lax.fori_loop(0,jnp.where(k==0,0,jnp.int32(64)),lp,0)
        def cbody(i,_):
            u=split(blk[i*nb+k])
            uh[i]=u[0]; ul[i]=u[1]
            c=dot3(u,(phi_o[k],plo_o[k]),NN)
            blk[i*nb+k]=c
            cs=split(c)
            ch[i]=cs[0]; cl[i]=cs[1]
            return 0
        lax.fori_loop(k+1,nr,cbody,0)
        def st(i,_):
            r=pl.ds(pl.multiple_of(i*W,W),W); c=pl.ds(pl.multiple_of(k*W,W),W)
            chi[r,c]=ch[i]; clo[r,c]=cl[i]
            return 0
        lax.fori_loop(k+1,nb,st,0)
        @pl.when(k+1<nb)
        def _():
            d=(k+1)*nb+k+1
            blk[d]=blk[d]-dot3((ch[k+1],cl[k+1]),(uh[k+1],ul[k+1]),NT)
        return 0
    lax.fori_loop(0,nb,step,0)
    o1=pltpu.make_async_copy(chi,chi_hbm,osem.at[0]); o2=pltpu.make_async_copy(clo,clo_hbm,osem.at[1])
    o1.start(); o2.start()
    for k in reversed(range(nb)):
        for e in range(extra):
            z=blk[(nb+e)*nb+k]
            for i in range(k+1,nb):
                cc=(chi[i*W:(i+1)*W,k*W:(k+1)*W],clo[i*W:(i+1)*W,k*W:(k+1)*W])
                xi=(blk_x(uh,ch,e,nb)[i], blk_x(ul,cl,e,nb)[i])
                z=z-dot3(xi,cc,NN)
            x=split(z)
            blk_x(uh,ch,e,nb)[k]=x[0]; blk_x(ul,cl,e,nb)[k]=x[1]
            s_o[e*W:(e+1)*W,k*W:(k+1)*W]=x[0]
    o1.wait(); o2.wait()
def blk_x(u,c,e,nb): return u if e==0 else c

def factor_call(a,g,interleave=True):
    n=a.shape[0]; nb=n//W; extra=g.shape[0]//W
    t=tables(nb,extra,64)
    sm=pl.BlockSpec(memory_space=pltpu.SMEM); an=pl.BlockSpec(memory_space=pl.ANY); vm=pl.BlockSpec(memory_space=pltpu.VMEM)
    return pl.pallas_call(
        functools.partial(factor_kernel,nb,extra,interleave),
        out_shape=(jax.ShapeDtypeStruct((n,n),bf),jax.ShapeDtypeStruct((n,n),bf),jax.ShapeDtypeStruct((nb,W,W),bf),jax.ShapeDtypeStruct((nb,W,W),bf),jax.ShapeDtypeStruct((extra*W,n),bf)),
        in_specs=[sm,sm,sm,an,an], out_specs=(an,an,vm,vm,vm),
        scratch_shapes=[pltpu.VMEM(((nb+extra)*nb,W,W),f32),pltpu.VMEM((n,n),bf),pltpu.VMEM((n,n),bf),
            pltpu.VMEM((nb+extra,W,W),bf),pltpu.VMEM((nb+extra,W,W),bf),pltpu.VMEM((nb+extra,W,W),bf),pltpu.VMEM((nb+extra,W,W),bf),
            pltpu.VMEM((3,128,128),f32),pltpu.SemaphoreType.DMA((nb,nb)),pltpu.SemaphoreType.DMA((extra,nb)),pltpu.SemaphoreType.DMA((2,))],
        compiler_params=pltpu.CompilerParams(vmem_limit_bytes=60*2**20),
        name="factor",
    )(*[jnp.asarray(x) for x in t],a,g)

def solve_kernel(nb, chi, clo, phi, plo, s_in, o, yh, yl):
    R=s_in.shape[0]
    for k in range(nb):
        y=s_in[:,k*W:(k+1)*W].astype(f32)
        if k:
            y=y-dot3((yh[:,:k*W],yl[:,:k*W]),(chi[k*W:(k+1)*W,:k*W],clo[k*W:(k+1)*W,:k*W]),NT)
        y=split(y)
        yh[:,k*W:(k+1)*W]=y[0]; yl[:,k*W:(k+1)*W]=y[1]
    for k in reversed(range(nb)):
        sl=slice(k*W,(k+1)*W)
        z=dot3((yh[:,sl],yl[:,sl]),(phi[k],plo[k]),NN)
        if k+1<nb:
            r=slice((k+1)*W,nb*W)
            z=z-dot3((yh[:,r],yl[:,r]),(chi[r,sl],clo[r,sl]),NN)
        x=split(z)
        yh[:,sl]=x[0]; yl[:,sl]=x[1]
        o[:,sl]=x[0]

def solve_call(chi,clo,phi,plo,s):
    n=chi.shape[0]; nb=n//W
    vm=pl.BlockSpec(memory_space=pltpu.VMEM)
    return pl.pallas_call(functools.partial(solve_kernel,nb),out_shape=jax.ShapeDtypeStruct(s.shape,bf),
        in_specs=[vm]*5,out_specs=vm,scratch_shapes=[pltpu.VMEM(s.shape,bf),pltpu.VMEM(s.shape,bf)],
        compiler_params=pltpu.CompilerParams(vmem_limit_bytes=60*2**20),name="solve")(chi,clo,phi,plo,s)

from jax.sharding import PartitionSpec as P

decay_rate = 0.5
damping = 0.1


def shifted(shard, axis, by):
    devices = lax.axis_size(axis)
    return lax.ppermute(shard, axis, [(i, (i + by) % devices) for i in range(devices)])


def per_device(features, previous, gradient):
    layers = lax.axis_size("factor") // 8
    shards = lax.axis_size("dp")
    factor_index = lax.axis_index("factor")
    layer_index = factor_index % layers
    member = factor_index // layers
    block_size = previous.shape[1]
    row_count = block_size // shards
    weight = (1.0 - decay_rate) / (features.shape[0] * shards)
    own_tokens = features[:, 0, :]
    start = lax.axis_index("dp") * row_count
    slot_ids = jnp.arange(2 * layers)
    slot_hot = jnp.where(slot_ids == 2 * layer_index + member % 2, 1.0, 0.0).astype(f32)
    stale = lax.dynamic_slice(previous[0], (start, start), (row_count, row_count))
    partial = weight * jnp.sum(jnp.square(own_tokens.astype(f32))) + decay_rate * jnp.trace(stale)
    traces = lax.psum(partial * slot_hot, ("dp", "factor"))
    input_trace = jnp.sum(jnp.where(slot_ids == 2 * layer_index, traces, 0.0))
    grad_trace = jnp.sum(jnp.where(slot_ids == 2 * layer_index + 1, traces, 0.0))
    pi_ratio = jnp.sqrt(input_trace / grad_trace)
    diag_shift = jnp.where(member % 2 == 0, pi_ratio, 1.0 / pi_ratio) * math.sqrt(damping)

    tokens = lax.all_gather(own_tokens, "dp", axis=0, tiled=True)
    gram = lax.dot_general(tokens, tokens, (((0,), (0,)), ((), ())), preferred_element_type=f32)
    factor = decay_rate * previous[0] + weight * gram
    own_rows = lax.dynamic_slice_in_dim(factor, start, row_count, 0)
    rows = lax.broadcasted_iota(jnp.int32, factor.shape, 0)
    cols = lax.broadcasted_iota(jnp.int32, factor.shape, 1)
    damped = factor + jnp.where(rows == cols, diag_shift, 0.0)

    tile_rows = gradient.shape[2]
    flat = gradient[0].reshape(2 * tile_rows, block_size).astype(f32)
    chi, clo, phi, plo, section_one = factor_call(damped, flat)
    section_one = section_one.reshape(2, tile_rows, block_size)
    moved = lax.all_to_all(section_one, "dp", split_axis=2, concat_axis=1, tiled=True)
    arrived = [shifted(moved[t], "factor", -layers * (2 * t + 1)) for t in range(2)]
    right = jnp.concatenate([a.T for a in arrived], axis=0)
    solved = solve_call(chi, clo, phi, plo, right)
    width = block_size // shards
    back = [shifted(solved[t * width : (t + 1) * width].T, "factor", layers * (2 * t + 1)) for t in range(2)]
    return (own_rows[None], jnp.stack(back)[None])


def solution(mesh):
    placed = (P("dp", "factor", None), P("factor", None, None), P("factor", None, "dp", None))
    return jax.shard_map(
        per_device,
        mesh=mesh,
        in_specs=placed,
        out_specs=(P("factor", "dp", None), P("factor", None, None, "dp")),
        check_vma=False,
    )
```

time: 2440 us -> 425 us (0.17)
  waiting for transfers between devices: 1050 us -> 69 us
  other arithmetic: 843 us -> 10.5 us
  matrix products: 265 us -> 30.2 us
  local copies, waits for them, and re-layouts: 202 us -> 12.8 us
  Pallas kernels: 0 us -> 140 us
  blocking collectives: 28.6 us -> 129 us
    another operation x90 -> x0, other arithmetic: 806 us -> none  [the longest x18 343 us: split_factor(): jax.scipy.linalg.solve_triangular(lower_tile, eye_tile, lower=True)]
    all_to_all x1 -> x0, waiting for transfers between devices: 655 us -> none  [per_device(): lax.all_to_all(section_one, 'dp', split_axis=3, concat_axis=2, tiled=True)]
    all_gather x1, waiting for transfers between devices: 205 us -> 5.11 us  [per_device(): tokens = lax.all_gather(own_tokens, 'dp', axis=0, tiled=True)]
    reduce_scatter x1 -> x0, waiting for transfers between devices: 191 us -> none  [per_device(): lax.psum_scatter(lax.dot_general(own_tokens, own_tokens, (((0,), (0,)), (...]
    dot_general x105 -> x1, matrix products: 211 us -> 30.2 us  [per_device(): lax.dot_general(tokens, tokens, (((0,), (0,)), ((), ())), preferred_eleme...]
    another operation x189 -> x0, local copies, waits for them, and re-layouts: 156 us -> none  [the longest x96 94.3 us: split_factor(): jax.scipy.linalg.solve_triangular(lower_tile, eye_tile, lower=True)]
    pallas_call x0 -> x2, Pallas kernels: none -> 140 us  [the longest x1 110 us: factor_call(): pl.pallas_call(functools.partial(factor_kernel, nb, extra, interleave), o...]
    psum x1, blocking collectives: 28.6 us -> 98.8 us  [per_device(): traces = lax.psum(partial * slot_hot, ('dp', 'factor'))]
  transfers between devices with their start and end apart: 5 -> 5, of which waited for: 3 -> 5; matrix products, arithmetic and copies ran while one was open for 16% -> 3% of each run, Pallas kernels for 0% -> 0%
where the time goes in v1:
time: 425 us; the launch traced here: 424 us
  Pallas kernels  140 us (33%)
  blocking collectives  129 us (30%)
  waiting for transfers between devices  69 us (16%)
  matrix products  30.2 us (7%)
  between operations  16.9 us (4%)
  starting transfers between devices  15.8 us (4%)
  local copies, waits for them, and re-layouts  12.8 us (3%)
  other arithmetic  10.5 us (2%)
    pallas_call x1, Pallas kernels, factor_call(): pl.pallas_call(functools.partial(factor_kernel, nb, extra, interleave), o...  110 us
    psum x1, blocking collectives, per_device(): traces = lax.psum(partial * slot_hot, ('dp', 'factor'))  98.8 us
    ppermute x4, waiting for transfers between devices, shifted(): lax.ppermute(shard, axis, [(i, (i + by) % devices) for i in range(devices)])  63.2 us
    all_to_all x1, blocking collectives, per_device(): lax.all_to_all(section_one, 'dp', split_axis=2, concat_axis=1, tiled=True)  30.7 us
    dot_general x1, matrix products, per_device(): lax.dot_general(tokens, tokens, (((0,), (0,)), ((), ())), preferred_eleme...  30.2 us
    pallas_call x1, Pallas kernels, solve_call(): pl.pallas_call(functools.partial(solve_kernel, nb), out_shape=jax.ShapeDt...  29.5 us
    ppermute x4, starting transfers between devices, shifted(): lax.ppermute(shard, axis, [(i, (i + by) % devices) for i in range(devices)])  15.7 us
  transfers between devices with their start and end apart: 5, of which 5 were waited for; matrix products, arithmetic and copies ran while one was open for 3% of the time, Pallas kernels for 0%

profile of v1, /device:TPU:0, one launch (start us, length us, event | category | flops | bytes accessed | tf_op | source)
XLA Modules:
  0.0 424.3 jit_solution(16451489120103712663)
XLA Ops:
  7.2 0.0 all-gather.3.cloned.1.call-start
  7.2 0.7 all-gather.3.cloned.1.call-update
  7.9 2.4 multiply_reduce_fusion
  11.0 1.6 fusion.1
  13.2 98.8 %psum.7 = f32[4]{0:T(128)S(1)} all-reduce(f32[4]{0:T(128)S(1)} %fusion.3), channel_id=1, replica_groups=mesh['dp'=8,'factor'=16] {'dp','factor'}, use_global_device_ids=true, to_apply=%region_2.3 | all-reduce | flops 4 | bytes 32 | tf_op jit(solution)/shard_map/psum | solution.py:224
  112.0 0.6 fusion.4
  114.0 4.2 bitcast_convert_fusion.g_hbm
  118.2 5.1 %all-gather.3.cloned.1.call-done = bf16[2048,1,2048]{2,0,1:T(8,128)(2,1)} async-done(((bf16[256,1,2048]{2,0,1:T(8,128)(2,1)}), bf16[2048,1,2048]{2,0,1:T(8,128)(2,1)}) %all-gather.3.cloned.1.call-update) | async-done | bytes 8388624 | tf_op jit(solution)/shard_map/all_gather | solution.py:230
  123.3 30.2 %select_add_fusion = (f32[2048,2048]{1,0:T(8,128)}, f32[2048,2048]{1,0:T(8,128)}) fusion(f32[]{:T(128)S(6)} %mul.49, bf16[2048,1,2048]{2,0,1:T(8,128)(2,1)} %all-gather.3.cloned.1.call-done, f32[1,2048,2048]{2,1,0:T(8,128)} %param.7), kind=kOutput, calls=%fused_computation.1 | convolution fusion | flops 17205035008 | bytes 58720260 | tf_op jit(solution)/shard_map/dot_general | solution.py:231
  153.5 110.2 %factor.1 = (bf16[2048,2048]{1,0:T(8,128)(2,1)}, bf16[2048,2048]{1,0:T(8,128)(2,1)}, bf16[8,256,256]{2,1,0:T(8,128)(2,1)}, bf16[8,256,256]{2,1,0:T(8,128)(2,1)}, bf16[512,2048]{1,0:T(8,128)(2,1)}) custom-call(s32[8,64]{1,0:T(8,128)} %constant.68.clone.dst_t, s32[8,64]{1,0:T(8,128)} %constant.69.clone.li_t, s32[8,64]{1,0:T(8,128)} %constant.70.clone.rj_t, ...), custom_call_target="tpu_custom_call" | custom-call | tf_op jit(solution)/shard_map/factor/pallas_call | solution.py:162
  263.8 4.8 %copy.13 = bf16[2,256,2048]{1,0,2:T(2,128)(2,1)S(1)} copy(bf16[2,256,2048]{2,1,0:T(8,128)(2,1)} %bitcast.45) | data formatting | bytes 4194304 | tf_op jit(solution)/shard_map/reshape | solution.py:241
  268.6 30.7 %all_to_all.15 = bf16[2,256,2048]{1,0,2:T(2,128)(2,1)S(1)} all-to-all(bf16[2,256,2048]{1,0,2:T(2,128)(2,1)S(1)} %copy.13), channel_id=1, replica_groups=mesh['dp'=8,'factor'=16] {'dp'}, dimensions={2} | all-to-all | bytes 4194304 | tf_op jit(solution)/shard_map/all_to_all | solution.py:242
  299.3 0.3 copy.14
  299.6 0.2 fusion.5
  299.8 0.1 copy.19
  299.9 1.6 collective-permute-start.1
  301.5 0.1 copy.18
  301.6 2.1 collective-permute-start
  303.7 21.0 %collective-permute-done.1 = bf16[2048,256]{0,1:T(8,128)(2,1)S(1)} collective-permute-done((bf16[2048,256]{0,1:T(8,128)(2,1)S(1)}, bf16[2048,256]{0,1:T(8,128)(2,1)S(1)}, u32[]{:S(2)}, u32[]{:S(2)}) %collective-permute-start.1) | collective-permute-done | bytes 1048608 | tf_op jit(solution)/shard_map/ppermute | solution.py:206
  324.7 13.2 %collective-permute-done = bf16[2048,256]{0,1:T(8,128)(2,1)S(1)} collective-permute-done((bf16[2048,256]{0,1:T(8,128)(2,1)S(1)}, bf16[2048,256]{0,1:T(8,128)(2,1)S(1)}, u32[]{:S(2)}, u32[]{:S(2)}) %collective-permute-start) | collective-permute-done | bytes 1048608 | tf_op jit(solution)/shard_map/ppermute | solution.py:206
  337.9 1.6 pad_maximum_fusion.s_in
  339.4 29.5 %solve.1 = bf16[512,2048]{1,0:T(8,128)(2,1)} custom-call(bf16[2048,2048]{1,0:T(8,128)(2,1)} %get-tuple-element.7.chi, bf16[2048,2048]{1,0:T(8,128)(2,1)} %get-tuple-element.8.clo, bf16[8,256,256]{2,1,0:T(8,128)(2,1)} %get-tuple-element.9.phi, bf16[8,256,256]{2,1,0:T(8,128)(2,1)} %get-tuple-element.10.plo, bf16[512,2048]{1,0:T(8,128)(2,1)} %pad_maximum_fusion.s_in), custom_call_target="tpu_custom_call" | custom-call | tf_op jit(solution)/shard_map/solve/pallas_call | solution.py:194
  368.9 1.7 slice_bitcast_fusion.1
  370.6 12.0 %collective-permute-start.3 = (bf16[2048,256]{0,1:T(8,128)(2,1)S(1)}, bf16[2048,256]{0,1:T(8,128)(2,1)S(1)}, u32[]{:S(2)}, u32[]{:S(2)}) collective-permute-start(bf16[2048,256]{0,1:T(8,128)(2,1)S(1)} %get-tuple-element.21), channel_id=1, source_target_pairs={{0,6},{1,7},{2,8},{3,9},{4,10},{5,11},{6,12},{7,13},{8,14},{9,15},... | collective-permute-start | bytes 3145736 | tf_op jit(solution)/shard_map/ppermute | solution.py:206
  382.6 0.0 collective-permute-start.2
  382.6 3.1 dynamic-slice_bitcast_fusion
  385.8 17.8 %collective-permute-done.3 = bf16[2048,256]{0,1:T(8,128)(2,1)S(1)} collective-permute-done((bf16[2048,256]{0,1:T(8,128)(2,1)S(1)}, bf16[2048,256]{0,1:T(8,128)(2,1)S(1)}, u32[]{:S(2)}, u32[]{:S(2)}) %collective-permute-start.3) | collective-permute-done | bytes 1048608 | tf_op jit(solution)/shard_map/ppermute | solution.py:206
  403.5 11.3 %collective-permute-done.2 = bf16[2048,256]{0,1:T(8,128)(2,1)S(1)} collective-permute-done((bf16[2048,256]{0,1:T(8,128)(2,1)S(1)}, bf16[2048,256]{0,1:T(8,128)(2,1)S(1)}, u32[]{:S(2)}, u32[]{:S(2)}) %collective-permute-start.2) | collective-permute-done | bytes 1048608 | tf_op jit(solution)/shard_map/ppermute | solution.py:206
  414.8 0.2 maximum_bitcast_fusion
  415.0 2.5 copy.17
  (1 shorter events, 0.0 us)
Async XLA Ops:
  7.2 116.2 %all-gather.3.cloned.1.call-start = ((), (), s32[]{:S(2)}) async-start(), calls=%async_computation.1 | async-start | bytes 9437184 | tf_op jit(solution)/shard_map/all_gather | solution.py:230
  299.9 24.8 %collective-permute-start.1 = (bf16[2048,256]{0,1:T(8,128)(2,1)S(1)}, bf16[2048,256]{0,1:T(8,128)(2,1)S(1)}, u32[]{:S(2)}, u32[]{:S(2)}) collective-permute-start(bf16[2048,256]{0,1:T(8,128)(2,1)S(1)} %bitcast.46), channel_id=1, source_target_pairs={{0,10},{1,11},{2,12},{3,13},{4,14},{5,15},{6,0},{7,1},{8,2},{9,3},... | collective-permute-start | bytes 3145736 | tf_op jit(solution)/shard_map/ppermute | solution.py:206
  301.6 36.2 %collective-permute-start = (bf16[2048,256]{0,1:T(8,128)(2,1)S(1)}, bf16[2048,256]{0,1:T(8,128)(2,1)S(1)}, u32[]{:S(2)}, u32[]{:S(2)}) collective-permute-start(bf16[2048,256]{0,1:T(8,128)(2,1)S(1)} %bitcast.47), channel_id=1, source_target_pairs={{0,14},{1,15},{2,0},{3,1},{4,2},{5,3},{6,4},{7,5},{8,6},{9,7},{10,... | collective-permute-start | bytes 3145736 | tf_op jit(solution)/shard_map/ppermute | solution.py:206
  370.6 32.9 %collective-permute-start.3 = (bf16[2048,256]{0,1:T(8,128)(2,1)S(1)}, bf16[2048,256]{0,1:T(8,128)(2,1)S(1)}, u32[]{:S(2)}, u32[]{:S(2)}) collective-permute-start(bf16[2048,256]{0,1:T(8,128)(2,1)S(1)} %get-tuple-element.21), channel_id=1, source_target_pairs={{0,6},{1,7},{2,8},{3,9},{4,10},{5,11},{6,12},{7,13},{8,14},{9,15},... | collective-permute-start | bytes 3145736 | tf_op jit(solution)/shard_map/ppermute | solution.py:206
  382.6 32.2 %collective-permute-start.2 = (bf16[2048,256]{0,1:T(8,128)(2,1)S(1)}, bf16[2048,256]{0,1:T(8,128)(2,1)S(1)}, u32[]{:S(2)}, u32[]{:S(2)}) collective-permute-start(bf16[2048,256]{0,1:T(8,128)(2,1)S(1)} %get-tuple-element.20), channel_id=1, source_target_pairs={{0,2},{1,3},{2,4},{3,5},{4,6},{5,7},{6,8},{7,9},{8,10},{9,11},{10,... | collective-permute-start | bytes 3145736 | tf_op jit(solution)/shard_map/ppermute | solution.py:206
Sparse Core Ops, SparseCore 0:
  10.3 112.9 all-gather.2

commit v2 on v1

v2 whole, which is shorter than its diff:
```python
import math
import jax, jax.numpy as jnp, numpy as np, functools
from jax import lax
from jax.experimental import pallas as pl
from jax.experimental.pallas import tpu as pltpu
W=256

def inv2(a,b,c):
    r = 1.0/(a*c-b*b)
    return c*r, -b*r, a*r

def inv4(p):
    a,b,c = inv2(p[0][0],p[0][1],p[1][1])
    b00,b01,b10,b11 = p[0][2],p[0][3],p[1][2],p[1][3]
    w00=a*b00+b*b10; w01=a*b01+b*b11; w10=b*b00+c*b10; w11=b*b01+c*b11
    s00=p[2][2]-(b00*w00+b10*w10); s01=p[2][3]-(b00*w01+b10*w11); s11=p[3][3]-(b01*w01+b11*w11)
    d00,d01,d11=inv2(s00,s01,s11)
    x00=-(w00*d00+w01*d01); x01=-(w00*d01+w01*d11); x10=-(w10*d00+w11*d01); x11=-(w10*d01+w11*d11)
    t00=a-(x00*w00+x01*w01); t01=b-(x00*w10+x01*w11); t11=c-(x10*w10+x11*w11)
    return [[t00,t01,x00,x01],[t01,t11,x10,x11],[x00,x10,d00,d01],[x01,x11,d01,d11]]

def invq(p,q):
    if q==1: return [[1.0/p[0][0]]]
    if q==2:
        a,b,c=inv2(p[0][0],p[0][1],p[1][1]); return [[a,b],[b,c]]
    return inv4(p)

NN=(((1,),(0,)),((),())); NT=(((1,),(1,)),((),()))
bf=jnp.bfloat16; f32=jnp.float32
def split(x):
    hi=x.astype(bf); return hi,(x-hi.astype(f32)).astype(bf)
def dot3(a,b,dims):
    d=lambda x,y: lax.dot_general(x,y,dims,preferred_element_type=f32)
    return d(a[0],b[0])+(d(a[0],b[1])+d(a[1],b[0]))

def sweep(A, slot, q=4, n=128):
    lane = lax.broadcasted_iota(jnp.int32,(1,n),1)
    for s in range(0,n,q):
        rows=[A[s+i:s+i+1,:] for i in range(q)]
        p=[[jnp.broadcast_to(rows[i][:,s+j:s+j+1],(1,n)) if j>=i else None for j in range(q)] for i in range(q)]
        X=invq(p,q)
        inl=(lane>=s)&(lane<s+q)
        rm=[jnp.where(lane==s+i,1.0,jnp.where(inl,0.0,rows[i])) for i in range(q)]
        nr=[]
        for i in range(q):
            t=X[i][0]*rm[0]
            for j in range(1,q): t=t+X[i][j]*rm[j]
            nr.append(t)
        tiles=[]
        for r in range(0,n,8):
            T=A[r:r+8,:]
            cols=[jnp.broadcast_to(T[:,s+i:s+i+1],(8,n)) for i in range(q)]
            T=jnp.where(inl,0.0,T)
            if r<=s<r+8:
                ri=lax.broadcasted_iota(jnp.int32,(8,1),0)+r
                inr=(ri>=s)&(ri<s+q)
                T=jnp.where(inr,0.0,T)
                cols=[jnp.where(ri==s+i,-1.0,jnp.where(inr,0.0,cols[i])) for i in range(q)]
            for i in range(q): T=T-cols[i]*nr[i]
            tiles.append(T)
        A=jnp.concatenate(tiles,axis=0)
        slot(s//q)
    return A

def tables(nb, extra, slots):
    dst=np.zeros((nb,slots),np.int32); li=np.zeros((nb,slots),np.int32); rj=np.zeros((nb,slots),np.int32)
    dst[:]=nb-1
    for k in range(1,nb):
        t=0
        for j in range(k,nb):
            for i in range(j,nb+extra):
                if (i,j)==(k,k): continue
                dst[k,t]=i*nb+j; li[k,t]=i; rj[k,t]=j; t+=1
        assert t<=slots
    return dst,li,rj

def factor_kernel(nb, extra, interleave, dst_t, li_t, rj_t, a_hbm, g_hbm, shift, chi_hbm, clo_hbm, phi_o, plo_o, s_o,
                  blk, chi, clo, uh, ul, ch, cl, half, asem, gsem, osem):
    nr=nb+extra
    first=[]; rest=[]
    for j in range(nb):
        for i in range(j,nb):
            c=pltpu.make_async_copy(a_hbm.at[i*nb+j], blk.at[i*nb+j], asem.at[i,j])
            (first if (i,j)==(0,0) else rest).append(c)
        for e in range(extra):
            rest.append(pltpu.make_async_copy(g_hbm.at[pl.ds(e*W,W),pl.ds(j*W,W)], blk.at[(nb+e)*nb+j], gsem.at[e,j]))
    for c in first+rest: c.start()
    for c in first: c.wait()
    eye=jnp.where(lax.broadcasted_iota(jnp.int32,(128,128),0)==lax.broadcasted_iota(jnp.int32,(128,128),1),shift[0:1,0:1],0.0)

    def tile(k,t):
        d=dst_t[k,t]; i=li_t[k,t]; j=rj_t[k,t]
        blk[d]=blk[d]-dot3((ch[i],cl[i]),(uh[j],ul[j]),NT)

    def step(k,_):
        kk=k*nb+k
        half[0]=blk[kk,:128,:128]+eye
        def hbody(h,_):
            fn=(lambda s: tile(k,h*32+s)) if interleave else (lambda s:None)
            p=sweep(half[h],fn)
            half[h]=p
            @pl.when((k==0)&(h==0))
            def _():
                for c in rest: c.wait()
            @pl.when(h==0)
            def _():
                d21=split(blk[kk,128:,:128])
                w=dot3(d21,split(p),NN)
                half[2]=w
                half[1]=(blk[kk,128:,128:]+eye)-dot3(split(w),d21,NT)
            return 0
        lax.fori_loop(0,2,hbody,0)
        p2=split(half[1]); w=half[2]
        x21=-dot3(p2,split(w),NN)
        wt=split(w.T)
        x11=half[0]-dot3(wt,split(x21),NN)
        x12=x21.T
        top=jnp.concatenate([x11,x12],axis=1)
        bot=jnp.concatenate([x21,half[1]],axis=1)
        P=split(jnp.concatenate([top,bot],axis=0))
        phi_o[k]=P[0]; plo_o[k]=P[1]
        if not interleave:
            def lp(t,_):
                tile(k,t); return 0
            lax.fori_loop(0,jnp.where(k==0,0,jnp.int32(64)),lp,0)
        def cbody(i,_):
            u=split(blk[i*nb+k])
            uh[i]=u[0]; ul[i]=u[1]
            c=dot3(u,(phi_o[k],plo_o[k]),NN)
            blk[i*nb+k]=c
            cs=split(c)
            ch[i]=cs[0]; cl[i]=cs[1]
            return 0
        lax.fori_loop(k+1,nr,cbody,0)
        def st(i,_):
            r=pl.ds(pl.multiple_of(i*W,W),W); c=pl.ds(pl.multiple_of(k*W,W),W)
            chi[r,c]=ch[i]; clo[r,c]=cl[i]
            return 0
        lax.fori_loop(k+1,nb,st,0)
        @pl.when(k+1<nb)
        def _():
            d=(k+1)*nb+k+1
            blk[d]=blk[d]-dot3((ch[k+1],cl[k+1]),(uh[k+1],ul[k+1]),NT)
        return 0
    lax.fori_loop(0,nb,step,0)
    o1=pltpu.make_async_copy(chi,chi_hbm,osem.at[0]); o2=pltpu.make_async_copy(clo,clo_hbm,osem.at[1])
    o1.start(); o2.start()
    for k in reversed(range(nb)):
        for e in range(extra):
            z=blk[(nb+e)*nb+k]
            for i in range(k+1,nb):
                cc=(chi[i*W:(i+1)*W,k*W:(k+1)*W],clo[i*W:(i+1)*W,k*W:(k+1)*W])
                xi=(blk_x(uh,ch,e,nb)[i], blk_x(ul,cl,e,nb)[i])
                z=z-dot3(xi,cc,NN)
            x=split(z)
            blk_x(uh,ch,e,nb)[k]=x[0]; blk_x(ul,cl,e,nb)[k]=x[1]
            s_o[k,e]=z.T.astype(bf)
    o1.wait(); o2.wait()
def blk_x(u,c,e,nb): return u if e==0 else c

def factor_call(a,g,shift,interleave=True):
    n=g.shape[1]; nb=n//W; extra=g.shape[0]//W
    t=tables(nb,extra,64)
    sm=pl.BlockSpec(memory_space=pltpu.SMEM); an=pl.BlockSpec(memory_space=pl.ANY); vm=pl.BlockSpec(memory_space=pltpu.VMEM)
    return pl.pallas_call(
        functools.partial(factor_kernel,nb,extra,interleave),
        out_shape=(jax.ShapeDtypeStruct((n,n),bf),jax.ShapeDtypeStruct((n,n),bf),jax.ShapeDtypeStruct((nb,W,W),bf),jax.ShapeDtypeStruct((nb,W,W),bf),jax.ShapeDtypeStruct((nb,extra,W,W),bf)),
        in_specs=[sm,sm,sm,an,an,vm], out_specs=(an,an,vm,vm,vm),
        scratch_shapes=[pltpu.VMEM(((nb+extra)*nb,W,W),f32),pltpu.VMEM((n,n),bf),pltpu.VMEM((n,n),bf),
            pltpu.VMEM((nb+extra,W,W),bf),pltpu.VMEM((nb+extra,W,W),bf),pltpu.VMEM((nb+extra,W,W),bf),pltpu.VMEM((nb+extra,W,W),bf),
            pltpu.VMEM((3,128,128),f32),pltpu.SemaphoreType.DMA((nb,nb)),pltpu.SemaphoreType.DMA((extra,nb)),pltpu.SemaphoreType.DMA((2,))],
        compiler_params=pltpu.CompilerParams(vmem_limit_bytes=60*2**20),
        name="factor",
    )(*[jnp.asarray(x) for x in t],a,g,shift)


from jax.sharding import PartitionSpec as P

decay_rate = 0.5
damping = 0.1

MESH = pl.DeviceIdType.MESH


def gather_kernel(dec, weight, damp, layers, own, prev, blocks, c_o, ft, acc, diag, part, tr1, tr2, zs, zr, t1s, t1r, t2s, t2r, psem, osem, lsem):
    dp = lax.axis_index("dp")
    f = lax.axis_index("factor")
    nb = 8
    z, y = dp // 4, dp % 4
    oz = 1 - z
    up, down = z * 4 + (y + 1) % 4, z * 4 + (y + 3) % 4
    member, layer = f // layers, f % layers
    far = z * 4 + (y + 2) % 4
    other, oup, odown, ofar = oz * 4 + y, oz * 4 + (y + 1) % 4, oz * 4 + (y + 3) % 4, oz * 4 + (y + 2) % 4

    loads = {}
    for i in range(nb):
        for j in range(i + 1):
            loads[i, j] = pltpu.make_async_copy(
                prev.at[0, pl.ds(i * W, W), pl.ds(j * W, W)], acc.at[i * nb + j], psem.at[i, j])
    row = pl.ds(pl.multiple_of(dp * W, W), W)
    dcopy = pltpu.make_async_copy(prev.at[0, row, row], diag, lsem.at[0])
    mine = pltpu.make_async_copy(own, ft.at[dp], lsem.at[1])
    dcopy.start()
    mine.start()

    barrier = pltpu.get_barrier_semaphore()
    for off in range(1, 8):
        pl.semaphore_signal(barrier, inc=1, device_id=((dp + off) % 8, f), device_id_type=MESH)
        pl.semaphore_signal(barrier, inc=1, device_id=(dp, ((member + off) % 8) * layers + layer), device_id_type=MESH)
    pl.semaphore_wait(barrier, 14)

    CH = zs.shape[0]
    rows = ft.shape[1] // CH
    half = rows // 2

    def send(kind, c, src, slot, to, lo, n):
        r = pl.ds(c * rows + lo, n)
        return pltpu.make_async_remote_copy(
            src_ref=src.at[r], dst_ref=ft.at[slot, r], send_sem=zs.at[c, kind], recv_sem=zr.at[c, kind],
            device_id=(to, f), device_id_type=MESH)

    cp = {}
    for c in range(CH):
        cp[0, c] = send(0, c, own, dp, other, 0, rows)
        cp[1, c] = send(1, c, own, dp, up, 0, rows)
        cp[2, c] = send(2, c, own, dp, down, 0, rows)
        cp[3, c] = send(3, c, ft.at[down], down, up, 0, half)
        cp[4, c] = send(4, c, ft.at[up], up, down, half, half)
        cp[5, c] = send(5, c, ft.at[other], other, up, 0, rows)
        cp[6, c] = send(6, c, ft.at[other], other, down, 0, rows)
        cp[7, c] = send(7, c, ft.at[odown], odown, up, 0, half)
        cp[8, c] = send(8, c, ft.at[oup], oup, down, half, half)
    for c in range(CH):
        for kind in range(3):
            cp[kind, c].start()

    dcopy.wait()
    ii = lax.broadcasted_iota(jnp.int32, (W, W), 0)
    jj = lax.broadcasted_iota(jnp.int32, (W, W), 1)
    tr = jnp.sum(jnp.where(ii == jj, diag[...], 0.0))
    xs = own[...].astype(f32)
    share = dec * tr + weight * jnp.sum(xs * xs)
    part[0] = jnp.full((8, 128), share, f32)
    tr1[dp] = part[0]
    c1 = [pltpu.make_async_remote_copy(
        src_ref=part.at[0], dst_ref=tr1.at[dp], send_sem=t1s.at[off], recv_sem=t1r.at[off],
        device_id=((dp + off) % 8, f), device_id_type=MESH) for off in range(1, 8)]
    for x in c1:
        x.start()
    for x in loads.values():
        x.start()
    for x in c1:
        x.wait()
    total = tr1[0]
    for i in range(1, 8):
        total = total + tr1[i]
    part[1] = total
    tr2[member] = total
    c2 = [pltpu.make_async_remote_copy(
        src_ref=part.at[1], dst_ref=tr2.at[member], send_sem=t2s.at[off], recv_sem=t2r.at[off],
        device_id=(dp, ((member + off) % 8) * layers + layer), device_id_type=MESH) for off in range(1, 8)]
    for x in c2:
        x.start()
    for x in loads.values():
        x.wait()
    mine.wait()

    per = nb // CH

    def tiles(c, slots, first):
        for i in range(c * per, (c + 1) * per):
            def body(j, _):
                d = None
                for s in slots:
                    t = lax.dot_general(ft[s, i * W:(i + 1) * W, :], ft[s, pl.ds(pl.multiple_of(j * W, W), W), :], NT, preferred_element_type=f32)
                    d = t if d is None else d + t
                old = acc[i * nb + j]
                acc[i * nb + j] = (dec * old if first else old) + weight * d
                return 0
            lax.fori_loop(0, i + 1, body, 0)

    for c in range(CH):
        cp[1, c].wait_recv()
        cp[3, c].start()
        cp[2, c].wait_recv()
        cp[4, c].start()
        cp[0, c].wait_recv()
        cp[5, c].start()
        cp[6, c].start()
        tiles(c, [dp, down, up, other], True)
    for x in c2:
        x.wait()
    s_in = tr2[0] + tr2[2] + tr2[4] + tr2[6]
    s_out = tr2[1] + tr2[3] + tr2[5] + tr2[7]
    ratio = jnp.sqrt(s_in / s_out)
    even = (jnp.full((8, 128), member, jnp.int32) % 2) == 0
    c_o[...] = jnp.where(even, ratio, 1.0 / ratio) * damp
    for c in range(CH):
        cp[5, c].wait_recv()
        cp[7, c].start()
        cp[6, c].wait_recv()
        cp[8, c].start()
        cp[3, c].wait_recv()
        cp[4, c].wait_recv()
        tiles(c, [odown, oup, far], False)
    outs = []
    for c in range(CH):
        cp[7, c].wait_recv()
        cp[8, c].wait_recv()
        tiles(c, [ofar], False)
        for i in range(c * per, (c + 1) * per):
            for j in range(i + 1):
                o = pltpu.make_async_copy(acc.at[i * nb + j], blocks.at[i * nb + j], osem.at[i, j])
                o.start()
                outs.append(o)
    for x in cp.values():
        x.wait_send()
    for o in outs:
        o.wait()


def gather_call(own, prev, layers, weight):
    n, w = own.shape
    nb = n // W
    CH = 4
    an = pl.BlockSpec(memory_space=pl.ANY)
    vm = pl.BlockSpec(memory_space=pltpu.VMEM)
    D = pltpu.SemaphoreType.DMA
    return pl.pallas_call(
        functools.partial(gather_kernel, decay_rate, weight, math.sqrt(damping), layers),
        out_shape=(jax.ShapeDtypeStruct((nb * nb, W, W), f32), jax.ShapeDtypeStruct((8, 128), f32)),
        in_specs=[vm, an], out_specs=(an, vm),
        scratch_shapes=[pltpu.VMEM((8, n, w), bf), pltpu.VMEM((nb * nb, W, W), f32), pltpu.VMEM((W, W), f32),
                        pltpu.VMEM((2, 8, 128), f32), pltpu.VMEM((8, 8, 128), f32), pltpu.VMEM((8, 8, 128), f32),
                        D((CH, 9)), D((CH, 9)), D((8,)), D((8,)), D((8,)), D((8,)), D((nb, nb)), D((nb, nb)), D((2,))],
        compiler_params=pltpu.CompilerParams(vmem_limit_bytes=56 * 2**20, collective_id=0, has_side_effects=True),
        cost_estimate=pl.CostEstimate(flops=10**10, bytes_accessed=3 * 10**7, transcendentals=0),
        name="gather_gram",
    )(own, prev)


def exchange_kernel(layers, s, blocks, chi_h, clo_h, phi_h, plo_h, out, rows_o,
                    chi, clo, phi, plo, arr, yh, yl, xb, rb, ss, sr, bs, br, csem, psem, rsem):
    dp = lax.axis_index("dp")
    f = lax.axis_index("factor")
    nf = lax.axis_size("factor")
    nb = chi.shape[0] // W
    to = [lax.rem(f + nf - layers * (2 * t + 1), nf) for t in range(2)]
    frm = [lax.rem(f + layers * (2 * t + 1), nf) for t in range(2)]
    barrier = pltpu.get_barrier_semaphore()
    for t in range(2):
        for off in range(8):
            pl.semaphore_signal(barrier, inc=1, device_id=(lax.rem(dp + off, 8), frm[t]), device_id_type=MESH)
            pl.semaphore_signal(barrier, inc=1, device_id=(lax.rem(dp + off, 8), to[t]), device_id_type=MESH)
    pl.semaphore_wait(barrier, 32)

    sends = []
    for off in range(8):
        for t in range(2):
            peer = lax.rem(dp + off, 8)
            x = pltpu.make_async_remote_copy(
                src_ref=s.at[peer, t], dst_ref=arr.at[dp, t], send_sem=ss.at[off, t], recv_sem=sr.at[dp, t],
                device_id=(peer, to[t]), device_id_type=MESH)
            x.start()
            sends.append(x)
    lp = [pltpu.make_async_copy(phi_h, phi, psem.at[0]), pltpu.make_async_copy(plo_h, plo, psem.at[1])]
    lc = {}
    for k in range(1, nb):
        a, b = slice(k * W, (k + 1) * W), slice(0, k * W)
        lc[k] = [pltpu.make_async_copy(chi_h.at[a, b], chi.at[a, b], csem.at[k, 0]),
                 pltpu.make_async_copy(clo_h.at[a, b], clo.at[a, b], csem.at[k, 1])]
    for k in range(1, nb):
        for x in lc[k]:
            x.start()
    for x in lp:
        x.start()
    lr = []
    for j in range(nb):
        idx = jnp.maximum(dp, j) * nb + jnp.minimum(dp, j)
        x = pltpu.make_async_copy(blocks.at[idx], rb.at[j], rsem.at[j])
        x.start()
        lr.append(x)
    for j in range(nb):
        lr[j].wait()
        v = rb[j]
        low = jnp.full((W, W), dp, jnp.int32) >= j
        rows_o[:, j * W:(j + 1) * W] = jnp.where(low, v, v.T)

    for k in range(nb):
        for t in range(2):
            pltpu.make_async_remote_copy(
                src_ref=s.at[k, t], dst_ref=arr.at[k, t], send_sem=ss.at[0, t], recv_sem=sr.at[k, t],
                device_id=(dp, to[t]), device_id_type=MESH).wait_recv()
        y = jnp.concatenate([arr[k, 0], arr[k, 1]], axis=0).astype(f32)
        if k:
            for x in lc[k]:
                x.wait()
            y = y - dot3((yh[:, :k * W], yl[:, :k * W]), (chi[k * W:(k + 1) * W, :k * W], clo[k * W:(k + 1) * W, :k * W]), NT)
        y = split(y)
        yh[:, k * W:(k + 1) * W] = y[0]
        yl[:, k * W:(k + 1) * W] = y[1]
    for x in lp:
        x.wait()
    backs = []
    for k in reversed(range(nb)):
        sl = slice(k * W, (k + 1) * W)
        zk = dot3((yh[:, sl], yl[:, sl]), (phi[k], plo[k]), NN)
        if k + 1 < nb:
            r = slice((k + 1) * W, nb * W)
            zk = zk - dot3((yh[:, r], yl[:, r]), (chi[r, sl], clo[r, sl]), NN)
        x = split(zk)
        yh[:, sl] = x[0]
        yl[:, sl] = x[1]
        for t in range(2):
            xb[k, t] = zk[t * W:(t + 1) * W].T.astype(bf)
            b = pltpu.make_async_remote_copy(
                src_ref=xb.at[k, t], dst_ref=out.at[t, pl.ds(k * W, W)], send_sem=bs.at[k, t], recv_sem=br.at[k, t],
                device_id=(dp, frm[t]), device_id_type=MESH)
            b.start()
            backs.append(b)
    for x in sends:
        x.wait_send()
    for b in backs:
        b.wait()


def exchange_call(s, blocks, chi, clo, phi, plo, layers):
    n = chi.shape[0]
    nb = n // W
    an = pl.BlockSpec(memory_space=pl.ANY)
    vm = pl.BlockSpec(memory_space=pltpu.VMEM)
    D = pltpu.SemaphoreType.DMA
    V = pltpu.VMEM
    return pl.pallas_call(
        functools.partial(exchange_kernel, layers),
        out_shape=(jax.ShapeDtypeStruct((2, n, W), bf), jax.ShapeDtypeStruct((W, n), f32)),
        in_specs=[vm] + [an] * 5, out_specs=(an, vm),
        scratch_shapes=[V((n, n), bf), V((n, n), bf), V((nb, W, W), bf), V((nb, W, W), bf), V((nb, 2, W, W), bf),
                        V((2 * W, n), bf), V((2 * W, n), bf), V((nb, 2, W, W), bf), V((nb, W, W), f32),
                        D((8, 2)), D((8, 2)), D((nb, 2)), D((nb, 2)), D((nb, 2)), D((2,)), D((nb,))],
        compiler_params=pltpu.CompilerParams(vmem_limit_bytes=56 * 2**20, collective_id=1, has_side_effects=True),
        cost_estimate=pl.CostEstimate(flops=13 * 10**9, bytes_accessed=3 * 10**7, transcendentals=0),
        name="exchange_solve",
    )(s, blocks, chi, clo, phi, plo)


def per_device(features, previous, gradient):
    layers = lax.axis_size("factor") // 8
    shards = lax.axis_size("dp")
    block_size = previous.shape[1]
    weight = (1.0 - decay_rate) / (features.shape[0] * shards)
    blocks, shift = gather_call(features[:, 0, :].T, previous, layers, weight)
    tile_rows = gradient.shape[2]
    flat = gradient[0].reshape(2 * tile_rows, block_size).astype(f32)
    chi, clo, phi, plo, section_one = factor_call(blocks, flat, shift)
    result, own_rows = exchange_call(section_one, blocks, chi, clo, phi, plo, layers)
    return (own_rows[None], result[None])


def solution(mesh):
    placed = (P("dp", "factor", None), P("factor", None, None), P("factor", None, "dp", None))
    return jax.shard_map(
        per_device,
        mesh=mesh,
        in_specs=placed,
        out_specs=(P("factor", "dp", None), P("factor", None, None, "dp")),
        check_vma=False,
    )
```

time: 425 us -> 303 us (0.71)
  Pallas kernels: 140 us -> 292 us
  blocking collectives: 129 us -> 0 us
  waiting for transfers between devices: 69 us -> 0 us
  matrix products: 30.2 us -> 0 us
  between operations: 16.9 us -> 0.67 us
  starting transfers between devices: 15.8 us -> 0 us
  other arithmetic: 10.5 us -> 2.72 us
  local copies, waits for them, and re-layouts: 12.8 us -> 7.02 us
    pallas_call x1 -> x2, Pallas kernels: 29.5 us -> 185 us  [the longest x1 95 us: exchange_call(): pl.pallas_call(functools.partial(exchange_kernel, layers), out_shape=(jax...]
    psum x1 -> x0, blocking collectives: 98.8 us -> none  [per_device(): traces = lax.psum(partial * slot_hot, ('dp', 'factor'))]
    ppermute x4 -> x0, waiting for transfers between devices: 63.2 us -> none  [shifted(): lax.ppermute(shard, axis, [(i, (i + by) % devices) for i in range(devices)])]
    all_to_all x1 -> x0, blocking collectives: 30.7 us -> none  [per_device(): lax.all_to_all(section_one, 'dp', split_axis=2, concat_axis=1, tiled=True)]
    dot_general x1 -> x0, matrix products: 30.2 us -> none  [per_device(): lax.dot_general(tokens, tokens, (((0,), (0,)), ((), ())), preferred_eleme...]
    ppermute x4 -> x0, starting transfers between devices: 15.7 us -> none  [shifted(): lax.ppermute(shard, axis, [(i, (i + by) % devices) for i in range(devices)])]
    all_gather x1 -> x0, waiting for transfers between devices: 5.11 us -> none  [per_device(): tokens = lax.all_gather(own_tokens, 'dp', axis=0, tiled=True)]
    reshape x1 -> x0, local copies, waits for them, and re-layouts: 4.83 us -> none  [per_device(): section_one = section_one.reshape(2, tile_rows, block_size)]
  transfers between devices with their start and end apart: 5 -> 0, of which waited for: 5 -> 0; matrix products, arithmetic and copies ran while one was open for 3% -> 0% of each run, Pallas kernels for 0% -> 0%
where the time goes in v2:
time: 303 us
  Pallas kernels  292 us (96%)
  local copies, waits for them, and re-layouts  7.02 us (2%)
    pallas_call x1, Pallas kernels, factor_call(): pl.pallas_call(functools.partial(factor_kernel, nb, extra, interleave), o...  107 us
    pallas_call x1, Pallas kernels, exchange_call(): pl.pallas_call(functools.partial(exchange_kernel, layers), out_shape=(jax...  95 us
    pallas_call x1, Pallas kernels, gather_call(): pl.pallas_call(functools.partial(gather_kernel, decay_rate, weight, math....  89.8 us
    unnamed x7, local copies, waits for them, and re-layouts  7.02 us

profile of v2, /device:TPU:0, one launch (start us, length us, event | category | flops | bytes accessed | tf_op | source)
XLA Modules:
  0.0 302.5 jit_solution(14572505553599747140)
XLA Ops:
  0.6 0.0 copy-start
  0.6 2.4 copy.8
  3.1 0.0 copy-done
  3.1 2.7 bitcast_convert_fusion.g_hbm
  5.8 89.8 %gather_gram.1 = (f32[64,256,256]{2,1,0:T(8,128)}, f32[8,128]{1,0:T(8,128)}) custom-call(bf16[2048,256]{1,0:T(8,128)(2,1)} %bitcast.10, f32[1,2048,2048]{2,1,0:T(8,128)} %prev.1), custom_call_target="tpu_custom_call" | custom-call | flops 10000000000 | bytes 30000000 | tf_op jit(solution)/shard_map/gather_gram/pallas_call | solution.py:330
  95.6 107.3 %factor.1 = (bf16[2048,2048]{1,0:T(8,128)(2,1)}, bf16[2048,2048]{1,0:T(8,128)(2,1)}, bf16[8,256,256]{2,1,0:T(8,128)(2,1)}, bf16[8,256,256]{2,1,0:T(8,128)(2,1)}, bf16[8,2,256,256]{3,2,1,0:T(8,128)(2,1)}) custom-call(s32[8,64]{1,0:T(8,128)} %constant.6.clone.dst_t, s32[8,64]{1,0:T(8,128)} %constant.7.clone.li_t, s32[8,64]{1,0:T(8,128)} %constant.8.clone.rj_t, ...), custom_call_target="tpu_custom_call" | custom-call | tf_op jit(solution)/shard_map/factor/pallas_call | solution.py:165
  202.9 95.0 %exchange_solve.1 = (bf16[2,2048,256]{2,1,0:T(8,128)(2,1)}, f32[256,2048]{1,0:T(8,128)}) custom-call(bf16[8,2,256,256]{3,2,1,0:T(8,128)(2,1)} %get-tuple-element.13.s, f32[64,256,256]{2,1,0:T(8,128)} %get-tuple-element.11.a_hbm.blocks, bf16[2048,2048]{1,0:T(8,128)(2,1)} %get-tuple-element.14.chi_h, bf16[2048,2048]{1,0:T(8,128)(2,1)} %get-tuple-element.15.clo_h, ...), custom_call_target="tpu_custom_call" | custom-call | flops 12999999488 | bytes 30000000 | tf_op jit(solution)/shard_map/exchange_solve/pallas_call | solution.py:435
  297.9 0.0 copy-start.1
  297.9 3.3 %copy.11 = f32[1,256,2048]{2,1,0:T(8,128)} copy(f32[1,256,2048]{2,1,0:T(8,128)} %bitcast.9) | data formatting | bytes 4194304
  301.2 0.0 copy-done.1
  301.2 1.3 copy.12
Async XLA Ops:
  0.6 2.4 copy-start
  297.9 3.3 %copy-start.1 = (bf16[2,2048,256]{2,1,0:T(8,128)(2,1)S(1)}, bf16[2,2048,256]{2,1,0:T(8,128)(2,1)}, u32[]{:S(2)}) copy-start(bf16[2,2048,256]{2,1,0:T(8,128)(2,1)} %get-tuple-element.19) | copy-start | bytes 6291460

commit v3 on v2

--- a/solution.py
+++ b/solution.py
@@ -75,15 +75,15 @@
     return dst,li,rj
 
 def factor_kernel(nb, extra, interleave, dst_t, li_t, rj_t, a_hbm, g_hbm, shift, chi_hbm, clo_hbm, phi_o, plo_o, s_o,
-                  blk, chi, clo, uh, ul, ch, cl, half, asem, gsem, osem):
+                  blk, gst, chi, clo, uh, ul, ch, cl, half, asem, gsem, osem):
     nr=nb+extra
+    cslots=nr-2
     first=[]; rest=[]
     for j in range(nb):
         for i in range(j,nb):
             c=pltpu.make_async_copy(a_hbm.at[i*nb+j], blk.at[i*nb+j], asem.at[i,j])
             (first if (i,j)==(0,0) else rest).append(c)
-        for e in range(extra):
-            rest.append(pltpu.make_async_copy(g_hbm.at[pl.ds(e*W,W),pl.ds(j*W,W)], blk.at[(nb+e)*nb+j], gsem.at[e,j]))
+    rest.append(pltpu.make_async_copy(g_hbm, gst, gsem.at[0]))
     for c in first+rest: c.start()
     for c in first: c.wait()
     eye=jnp.where(lax.broadcasted_iota(jnp.int32,(128,128),0)==lax.broadcasted_iota(jnp.int32,(128,128),1),shift[0:1,0:1],0.0)
@@ -92,83 +92,80 @@
         d=dst_t[k,t]; i=li_t[k,t]; j=rj_t[k,t]
         blk[d]=blk[d]-dot3((ch[i],cl[i]),(uh[j],ul[j]),NT)
 
+    def panel(i,k):
+        u=split(blk[i*nb+k])
+        uh[i]=u[0]; ul[i]=u[1]
+        c=split(dot3(u,(phi_o[k],plo_o[k]),NN))
+        ch[i]=c[0]; cl[i]=c[1]
+        r=pl.ds(pl.multiple_of(i*W,W),W); cc=pl.ds(pl.multiple_of(k*W,W),W)
+        chi[r,cc]=c[0]; clo[r,cc]=c[1]
+
     def step(k,_):
         kk=k*nb+k
-        half[0]=blk[kk,:128,:128]+eye
-        def hbody(h,_):
-            fn=(lambda s: tile(k,h*32+s)) if interleave else (lambda s:None)
-            p=sweep(half[h],fn)
-            half[h]=p
-            @pl.when((k==0)&(h==0))
-            def _():
-                for c in rest: c.wait()
-            @pl.when(h==0)
-            def _():
-                d21=split(blk[kk,128:,:128])
-                w=dot3(d21,split(p),NN)
-                half[2]=w
-                half[1]=(blk[kk,128:,128:]+eye)-dot3(split(w),d21,NT)
-            return 0
-        lax.fori_loop(0,2,hbody,0)
-        p2=split(half[1]); w=half[2]
+        kp=jnp.maximum(k-1,0)
+        def slot(h,s):
+            if not interleave: return
+            if h==0 and s<cslots: panel(jnp.minimum(k+1+s,nr-1),kp)
+            else: tile(k,h*32+s-cslots)
+        p1=sweep(blk[kk,:128,:128]+eye,lambda s: slot(0,s))
+        half[0]=p1
+        @pl.when(k==0)
+        def _():
+            for c in rest: c.wait()
+            for j in range(nb):
+                for e in range(extra):
+                    blk[(nb+e)*nb+j]=gst[e*W:(e+1)*W,j*W:(j+1)*W].astype(f32)
+        d21=split(blk[kk,128:,:128])
+        w=dot3(d21,split(half[0]),NN)
+        sw=split(w)
+        half[2]=w
+        p2v=sweep((blk[kk,128:,128:]+eye)-dot3(sw,d21,NT),lambda s: slot(1,s))
+        p2=split(p2v); w=half[2]
         x21=-dot3(p2,split(w),NN)
-        wt=split(w.T)
-        x11=half[0]-dot3(wt,split(x21),NN)
-        x12=x21.T
-        top=jnp.concatenate([x11,x12],axis=1)
-        bot=jnp.concatenate([x21,half[1]],axis=1)
+        x11=half[0]-dot3(split(w.T),split(x21),NN)
+        top=jnp.concatenate([x11,x21.T],axis=1)
+        bot=jnp.concatenate([x21,p2v],axis=1)
         P=split(jnp.concatenate([top,bot],axis=0))
         phi_o[k]=P[0]; plo_o[k]=P[1]
         if not interleave:
             def lp(t,_):
                 tile(k,t); return 0
             lax.fori_loop(0,jnp.where(k==0,0,jnp.int32(64)),lp,0)
-        def cbody(i,_):
-            u=split(blk[i*nb+k])
-            uh[i]=u[0]; ul[i]=u[1]
-            c=dot3(u,(phi_o[k],plo_o[k]),NN)
-            blk[i*nb+k]=c
-            cs=split(c)
-            ch[i]=cs[0]; cl[i]=cs[1]
-            return 0
-        lax.fori_loop(k+1,nr,cbody,0)
-        def st(i,_):
-            r=pl.ds(pl.multiple_of(i*W,W),W); c=pl.ds(pl.multiple_of(k*W,W),W)
-            chi[r,c]=ch[i]; clo[r,c]=cl[i]
-            return 0
-        lax.fori_loop(k+1,nb,st,0)
+            def lc(i,_):
+                panel(i,k); return 0
+            lax.fori_loop(k+2,nr,lc,0)
+        panel(k+1,k)
         @pl.when(k+1<nb)
         def _():
             d=(k+1)*nb+k+1
             blk[d]=blk[d]-dot3((ch[k+1],cl[k+1]),(uh[k+1],ul[k+1]),NT)
         return 0
     lax.fori_loop(0,nb,step,0)
-    o1=pltpu.make_async_copy(chi,chi_hbm,osem.at[0]); o2=pltpu.make_async_copy(clo,clo_hbm,osem.at[1])
+    o1=pltpu.make_async_copy(chi.at[pl.ds(0,nb*W)],chi_hbm,osem.at[0]); o2=pltpu.make_async_copy(clo.at[pl.ds(0,nb*W)],clo_hbm,osem.at[1])
     o1.start(); o2.start()
+    for i in range(nb+1,nr): panel(i,nb-1)
+    er=slice(nb*W,nr*W)
     for k in reversed(range(nb)):
-        for e in range(extra):
-            z=blk[(nb+e)*nb+k]
-            for i in range(k+1,nb):
-                cc=(chi[i*W:(i+1)*W,k*W:(k+1)*W],clo[i*W:(i+1)*W,k*W:(k+1)*W])
-                xi=(blk_x(uh,ch,e,nb)[i], blk_x(ul,cl,e,nb)[i])
-                z=z-dot3(xi,cc,NN)
-            x=split(z)
-            blk_x(uh,ch,e,nb)[k]=x[0]; blk_x(ul,cl,e,nb)[k]=x[1]
-            s_o[k,e]=z.T.astype(bf)
+        sl=slice(k*W,(k+1)*W)
+        z=chi[er,sl].astype(f32)+clo[er,sl].astype(f32)
+        if k+1<nb:
+            b=slice((k+1)*W,nb*W)
+            z=z-dot3((chi[er,b],clo[er,b]),(chi[b,sl],clo[b,sl]),NN)
+        x=split(z)
+        chi[er,sl]=x[0]; clo[er,sl]=x[1]
+        for e in range(extra): s_o[k,e]=z[e*W:(e+1)*W].T.astype(bf)
     o1.wait(); o2.wait()
-def blk_x(u,c,e,nb): return u if e==0 else c
-
 def factor_call(a,g,shift,interleave=True):
     n=g.shape[1]; nb=n//W; extra=g.shape[0]//W
-    t=tables(nb,extra,64)
+    t=tables(nb,extra,64-(nb+extra-2))
     sm=pl.BlockSpec(memory_space=pltpu.SMEM); an=pl.BlockSpec(memory_space=pl.ANY); vm=pl.BlockSpec(memory_space=pltpu.VMEM)
     return pl.pallas_call(
         functools.partial(factor_kernel,nb,extra,interleave),
         out_shape=(jax.ShapeDtypeStruct((n,n),bf),jax.ShapeDtypeStruct((n,n),bf),jax.ShapeDtypeStruct((nb,W,W),bf),jax.ShapeDtypeStruct((nb,W,W),bf),jax.ShapeDtypeStruct((nb,extra,W,W),bf)),
         in_specs=[sm,sm,sm,an,an,vm], out_specs=(an,an,vm,vm,vm),
-        scratch_shapes=[pltpu.VMEM(((nb+extra)*nb,W,W),f32),pltpu.VMEM((n,n),bf),pltpu.VMEM((n,n),bf),
+        scratch_shapes=[pltpu.VMEM(((nb+extra)*nb,W,W),f32),pltpu.VMEM((extra*W,n),bf),pltpu.VMEM((n+extra*W,n),bf),pltpu.VMEM((n+extra*W,n),bf),
             pltpu.VMEM((nb+extra,W,W),bf),pltpu.VMEM((nb+extra,W,W),bf),pltpu.VMEM((nb+extra,W,W),bf),pltpu.VMEM((nb+extra,W,W),bf),
-            pltpu.VMEM((3,128,128),f32),pltpu.SemaphoreType.DMA((nb,nb)),pltpu.SemaphoreType.DMA((extra,nb)),pltpu.SemaphoreType.DMA((2,))],
+            pltpu.VMEM((3,128,128),f32),pltpu.SemaphoreType.DMA((nb,nb)),pltpu.SemaphoreType.DMA((1,)),pltpu.SemaphoreType.DMA((2,))],
         compiler_params=pltpu.CompilerParams(vmem_limit_bytes=60*2**20),
         name="factor",
     )(*[jnp.asarray(x) for x in t],a,g,shift)
@@ -227,10 +224,12 @@
         cp[2, c] = send(2, c, own, dp, down, 0, rows)
         cp[3, c] = send(3, c, ft.at[down], down, up, 0, half)
         cp[4, c] = send(4, c, ft.at[up], up, down, half, half)
-        cp[5, c] = send(5, c, ft.at[other], other, up, 0, rows)
-        cp[6, c] = send(6, c, ft.at[other], other, down, 0, rows)
+        cp[5, c] = send(5, c, ft.at[other], other, up, 0, half)
+        cp[6, c] = send(6, c, ft.at[other], other, down, half, half)
         cp[7, c] = send(7, c, ft.at[odown], odown, up, 0, half)
         cp[8, c] = send(8, c, ft.at[oup], oup, down, half, half)
+        cp[9, c] = send(9, c, ft.at[down], down, other, half, half)
+        cp[10, c] = send(10, c, ft.at[up], up, other, 0, half)
     for c in range(CH):
         for kind in range(3):
             cp[kind, c].start()
@@ -262,9 +261,6 @@
         device_id=(dp, ((member + off) % 8) * layers + layer), device_id_type=MESH) for off in range(1, 8)]
     for x in c2:
         x.start()
-    for x in loads.values():
-        x.wait()
-    mine.wait()
 
     per = nb // CH
 
@@ -283,11 +279,17 @@
     for c in range(CH):
         cp[1, c].wait_recv()
         cp[3, c].start()
+        cp[9, c].start()
         cp[2, c].wait_recv()
         cp[4, c].start()
+        cp[10, c].start()
         cp[0, c].wait_recv()
         cp[5, c].start()
         cp[6, c].start()
+    for x in loads.values():
+        x.wait()
+    mine.wait()
+    for c in range(CH):
         tiles(c, [dp, down, up, other], True)
     for x in c2:
         x.wait()
@@ -301,8 +303,9 @@
         cp[7, c].start()
         cp[6, c].wait_recv()
         cp[8, c].start()
-        cp[3, c].wait_recv()
-        cp[4, c].wait_recv()
+    for c in range(CH):
+        for kind in (3, 4, 9, 10):
+            cp[kind, c].wait_recv()
         tiles(c, [odown, oup, far], False)
     outs = []
     for c in range(CH):
@@ -333,7 +336,7 @@
         in_specs=[vm, an], out_specs=(an, vm),
         scratch_shapes=[pltpu.VMEM((8, n, w), bf), pltpu.VMEM((nb * nb, W, W), f32), pltpu.VMEM((W, W), f32),
                         pltpu.VMEM((2, 8, 128), f32), pltpu.VMEM((8, 8, 128), f32), pltpu.VMEM((8, 8, 128), f32),
-                        D((CH, 9)), D((CH, 9)), D((8,)), D((8,)), D((8,)), D((8,)), D((nb, nb)), D((nb, nb)), D((2,))],
+                        D((CH, 11)), D((CH, 11)), D((8,)), D((8,)), D((8,)), D((8,)), D((nb, nb)), D((nb, nb)), D((2,))],
         compiler_params=pltpu.CompilerParams(vmem_limit_bytes=56 * 2**20, collective_id=0, has_side_effects=True),
         cost_estimate=pl.CostEstimate(flops=10**10, bytes_accessed=3 * 10**7, transcendentals=0),
         name="gather_gram",
@@ -341,7 +344,7 @@
 
 
 def exchange_kernel(layers, s, blocks, chi_h, clo_h, phi_h, plo_h, out, rows_o,
-                    chi, clo, phi, plo, arr, yh, yl, xb, rb, ss, sr, bs, br, csem, psem, rsem):
+                    chi, clo, phi, plo, arr, yh, yl, xb, rl, rb, ss, sr, bs, br, rs, rr, csem, psem, rsem):
     dp = lax.axis_index("dp")
     f = lax.axis_index("factor")
     nf = lax.axis_size("factor")
@@ -353,17 +356,21 @@
         for off in range(8):
             pl.semaphore_signal(barrier, inc=1, device_id=(lax.rem(dp + off, 8), frm[t]), device_id_type=MESH)
             pl.semaphore_signal(barrier, inc=1, device_id=(lax.rem(dp + off, 8), to[t]), device_id_type=MESH)
-    pl.semaphore_wait(barrier, 32)
-
-    sends = []
-    for off in range(8):
-        for t in range(2):
-            peer = lax.rem(dp + off, 8)
-            x = pltpu.make_async_remote_copy(
-                src_ref=s.at[peer, t], dst_ref=arr.at[dp, t], send_sem=ss.at[off, t], recv_sem=sr.at[dp, t],
-                device_id=(peer, to[t]), device_id_type=MESH)
-            x.start()
-            sends.append(x)
+    pl.semaphore_signal(barrier, inc=1, device_id=(dp, lax.rem(f + nf // 2, nf)), device_id_type=MESH)
+    pl.semaphore_wait(barrier, 33)
+
+    H = W // 2
+
+    def part(g, off, t):
+        peer = lax.rem(dp + off, 8)
+        r = pl.ds(g * H, H)
+        return pltpu.make_async_remote_copy(
+            src_ref=s.at[peer, t, r], dst_ref=arr.at[dp, t, r], send_sem=ss.at[g, off, t], recv_sem=sr.at[g, dp, t],
+            device_id=(peer, to[t]), device_id_type=MESH)
+
+    sends = [[part(g, off, t) for off in range(8) for t in range(2)] for g in range(2)]
+    for x in sends[0]:
+        x.start()
     lp = [pltpu.make_async_copy(phi_h, phi, psem.at[0]), pltpu.make_async_copy(plo_h, plo, psem.at[1])]
     lc = {}
     for k in range(1, nb):
@@ -387,42 +394,90 @@
         low = jnp.full((W, W), dp, jnp.int32) >= j
         rows_o[:, j * W:(j + 1) * W] = jnp.where(low, v, v.T)
 
-    for k in range(nb):
+    for x in sends[0]:
+        x.wait_send()
+    for x in sends[1]:
+        x.start()
+    edge = lax.rem(f // layers, 4) == 3
+
+    def home(g, k, t, to_f):
+        return pltpu.make_async_remote_copy(
+            src_ref=xb.at[g, k, t], dst_ref=out.at[t, pl.ds(k * W, W), pl.ds(g * H, H)],
+            send_sem=bs.at[g, k, t], recv_sem=br.at[g, k, t], device_id=(dp, to_f), device_id_type=MESH)
+
+    def hop(g, k):
+        return pltpu.make_async_remote_copy(
+            src_ref=xb.at[g, k, 0], dst_ref=rl.at[g, k], send_sem=bs.at[g, k, 0], recv_sem=rr.at[g, k],
+            device_id=(dp, lax.rem(f + nf // 2, nf)), device_id_type=MESH)
+
+    def onward(g, k):
+        return pltpu.make_async_remote_copy(
+            src_ref=rl.at[g, k], dst_ref=out.at[0, pl.ds(k * W, W), pl.ds(g * H, H)],
+            send_sem=rs.at[g, k], recv_sem=br.at[g, k, 0],
+            device_id=(dp, lax.rem(f + layers + nf // 2, nf)), device_id_type=MESH)
+
+    def relay(g, k):
+        @pl.when(edge)
+        def _():
+            hop(g, k).wait_recv()
+            onward(g, k).start()
+
+    order = []
+    for g in range(2):
+        r = slice(g * H, (g + 1) * H)
+        for k in range(nb):
+            for t in range(2):
+                pltpu.make_async_remote_copy(
+                    src_ref=s.at[k, t, r], dst_ref=arr.at[k, t, r], send_sem=ss.at[g, 0, t], recv_sem=sr.at[g, k, t],
+                    device_id=(dp, to[t]), device_id_type=MESH).wait_recv()
+            y = jnp.concatenate([arr[k, 0, r], arr[k, 1, r]], axis=0).astype(f32)
+            if k:
+                if g == 0:
+                    for x in lc[k]:
+                        x.wait()
+                b = slice(0, k * W)
+                c = slice(k * W, (k + 1) * W)
+                y = y - dot3((yh[g, :, b], yl[g, :, b]), (chi[c, b], clo[c, b]), NT)
+            y = split(y)
+            yh[g, :, k * W:(k + 1) * W] = y[0]
+            yl[g, :, k * W:(k + 1) * W] = y[1]
+        if g == 0:
+            for x in lp:
+                x.wait()
+        for k in reversed(range(nb)):
+            sl = slice(k * W, (k + 1) * W)
+            zk = dot3((yh[g, :, sl], yl[g, :, sl]), (phi[k], plo[k]), NN)
+            if k + 1 < nb:
+                b = slice((k + 1) * W, nb * W)
+                zk = zk - dot3((yh[g, :, b], yl[g, :, b]), (chi[b, sl], clo[b, sl]), NN)
+            x = split(zk)
+            yh[g, :, sl] = x[0]
+            yl[g, :, sl] = x[1]
+            for t in range(2):
+                xb[g, k, t] = zk[t * H:(t + 1) * H].T.astype(bf)
+            home(g, k, 1, frm[1]).start()
+
+            @pl.when(edge)
+            def _():
+                hop(g, k).start()
+
+            @pl.when(jnp.logical_not(edge))
+            def _():
+                home(g, k, 0, frm[0]).start()
+
+            order.append((g, k))
+            if len(order) > 1:
+                relay(*order[-2])
+    relay(*order[-1])
+    for x in sends[1]:
+        x.wait_send()
+    for g, k in order:
         for t in range(2):
-            pltpu.make_async_remote_copy(
-                src_ref=s.at[k, t], dst_ref=arr.at[k, t], send_sem=ss.at[0, t], recv_sem=sr.at[k, t],
-                device_id=(dp, to[t]), device_id_type=MESH).wait_recv()
-        y = jnp.concatenate([arr[k, 0], arr[k, 1]], axis=0).astype(f32)
-        if k:
-            for x in lc[k]:
-                x.wait()
-            y = y - dot3((yh[:, :k * W], yl[:, :k * W]), (chi[k * W:(k + 1) * W, :k * W], clo[k * W:(k + 1) * W, :k * W]), NT)
-        y = split(y)
-        yh[:, k * W:(k + 1) * W] = y[0]
-        yl[:, k * W:(k + 1) * W] = y[1]
-    for x in lp:
-        x.wait()
-    backs = []
-    for k in reversed(range(nb)):
-        sl = slice(k * W, (k + 1) * W)
-        zk = dot3((yh[:, sl], yl[:, sl]), (phi[k], plo[k]), NN)
-        if k + 1 < nb:
-            r = slice((k + 1) * W, nb * W)
-            zk = zk - dot3((yh[:, r], yl[:, r]), (chi[r, sl], clo[r, sl]), NN)
-        x = split(zk)
-        yh[:, sl] = x[0]
-        yl[:, sl] = x[1]
-        for t in range(2):
-            xb[k, t] = zk[t * W:(t + 1) * W].T.astype(bf)
-            b = pltpu.make_async_remote_copy(
-                src_ref=xb.at[k, t], dst_ref=out.at[t, pl.ds(k * W, W)], send_sem=bs.at[k, t], recv_sem=br.at[k, t],
-                device_id=(dp, frm[t]), device_id_type=MESH)
-            b.start()
-            backs.append(b)
-    for x in sends:
-        x.wait_send()
-    for b in backs:
-        b.wait()
+            home(g, k, t, frm[t]).wait()
+
+        @pl.when(edge)
+        def _():
+            onward(g, k).wait_send()
 
 
 def exchange_call(s, blocks, chi, clo, phi, plo, layers):
@@ -437,8 +492,8 @@
         out_shape=(jax.ShapeDtypeStruct((2, n, W), bf), jax.ShapeDtypeStruct((W, n), f32)),
         in_specs=[vm] + [an] * 5, out_specs=(an, vm),
         scratch_shapes=[V((n, n), bf), V((n, n), bf), V((nb, W, W), bf), V((nb, W, W), bf), V((nb, 2, W, W), bf),
-                        V((2 * W, n), bf), V((2 * W, n), bf), V((nb, 2, W, W), bf), V((nb, W, W), f32),
-                        D((8, 2)), D((8, 2)), D((nb, 2)), D((nb, 2)), D((nb, 2)), D((2,)), D((nb,))],
+                        V((2, W, n), bf), V((2, W, n), bf), V((2, nb, 2, W, W // 2), bf), V((2, nb, W, W // 2), bf), V((nb, W, W), f32),
+                        D((2, 8, 2)), D((2, 8, 2)), D((2, nb, 2)), D((2, nb, 2)), D((2, nb)), D((2, nb)), D((nb, 2)), D((2,)), D((nb,))],
         compiler_params=pltpu.CompilerParams(vmem_limit_bytes=56 * 2**20, collective_id=1, has_side_effects=True),
         cost_estimate=pl.CostEstimate(flops=13 * 10**9, bytes_accessed=3 * 10**7, transcendentals=0),
         name="exchange_solve",
@@ -452,7 +507,7 @@
     weight = (1.0 - decay_rate) / (features.shape[0] * shards)
     blocks, shift = gather_call(features[:, 0, :].T, previous, layers, weight)
     tile_rows = gradient.shape[2]
-    flat = gradient[0].reshape(2 * tile_rows, block_size).astype(f32)
+    flat = gradient[0].reshape(2 * tile_rows, block_size)
     chi, clo, phi, plo, section_one = factor_call(blocks, flat, shift)
     result, own_rows = exchange_call(section_one, blocks, chi, clo, phi, plo, layers)
     return (own_rows[None], result[None])

time: 303 us -> 283 us (0.934); the launches traced: 303 us -> 278 us
  Pallas kernels: 292 us -> 270 us
    pallas_call x1, Pallas kernels: 95 us -> 82.4 us  [exchange_call(): pl.pallas_call(functools.partial(exchange_kernel, layers), out_shape=(jax...]
    pallas_call x1, Pallas kernels: 89.8 us -> 84.2 us  [gather_call(): pl.pallas_call(functools.partial(gather_kernel, decay_rate, weight, math....]
    pallas_call x1, Pallas kernels: 107 us -> 104 us  [factor_call(): pl.pallas_call(functools.partial(factor_kernel, nb, extra, interleave), o...]
    unnamed x7 -> x5, local copies, waits for them, and re-layouts: 7.02 us -> 6.87 us
where the time goes in v3:
time: 283 us; the launch traced here: 278 us
  Pallas kernels  270 us (95%)
  local copies, waits for them, and re-layouts  6.87 us (2%)
    pallas_call x1, Pallas kernels, factor_call(): pl.pallas_call(functools.partial(factor_kernel, nb, extra, interleave), o...  104 us
    pallas_call x1, Pallas kernels, gather_call(): pl.pallas_call(functools.partial(gather_kernel, decay_rate, weight, math....  84.2 us
    pallas_call x1, Pallas kernels, exchange_call(): pl.pallas_call(functools.partial(exchange_kernel, layers), out_shape=(jax...  82.4 us
    unnamed x5, local copies, waits for them, and re-layouts  6.87 us

profile of v3, /device:TPU:0, one launch (start us, length us, event | category | flops | bytes accessed | tf_op | source)
XLA Modules:
  0.0 278.1 jit_solution(4420790799421120996)
XLA Ops:
  0.6 2.3 copy.8
  2.9 84.2 %gather_gram.1 = (f32[64,256,256]{2,1,0:T(8,128)}, f32[8,128]{1,0:T(8,128)}) custom-call(bf16[2048,256]{1,0:T(8,128)(2,1)} %bitcast.9, f32[1,2048,2048]{2,1,0:T(8,128)} %prev.1), custom_call_target="tpu_custom_call" | custom-call | flops 10000000000 | bytes 30000000 | tf_op jit(solution)/shard_map/gather_gram/pallas_call | solution.py:333
  87.1 103.7 %factor.1 = (bf16[2048,2048]{1,0:T(8,128)(2,1)}, bf16[2048,2048]{1,0:T(8,128)(2,1)}, bf16[8,256,256]{2,1,0:T(8,128)(2,1)}, bf16[8,256,256]{2,1,0:T(8,128)(2,1)}, bf16[8,2,256,256]{3,2,1,0:T(8,128)(2,1)}) custom-call(s32[8,56]{1,0:T(8,128)} %constant.6.clone.dst_t, s32[8,56]{1,0:T(8,128)} %constant.7.clone.li_t, s32[8,56]{1,0:T(8,128)} %constant.8.clone.rj_t, ...), custom_call_target="tpu_custom_call" | custom-call | tf_op jit(solution)/shard_map/factor/pallas_call | solution.py:162
  190.8 82.4 %exchange_solve.1 = (bf16[2,2048,256]{2,1,0:T(8,128)(2,1)}, f32[256,2048]{1,0:T(8,128)}) custom-call(bf16[8,2,256,256]{3,2,1,0:T(8,128)(2,1)} %get-tuple-element.13.s, f32[64,256,256]{2,1,0:T(8,128)} %get-tuple-element.11.a_hbm.blocks, bf16[2048,2048]{1,0:T(8,128)(2,1)} %get-tuple-element.14.chi_h, bf16[2048,2048]{1,0:T(8,128)(2,1)} %get-tuple-element.15.clo_h, ...), custom_call_target="tpu_custom_call" | custom-call | flops 12999999488 | bytes 30000000 | tf_op jit(solution)/shard_map/exchange_solve/pallas_call | solution.py:490
  273.2 0.0 copy-start
  273.2 3.3 %copy.11 = f32[1,256,2048]{2,1,0:T(8,128)} copy(f32[1,256,2048]{2,1,0:T(8,128)} %bitcast.7) | data formatting | bytes 4194304
  276.5 0.0 copy-done
  276.5 1.3 copy.12
Async XLA Ops:
  273.2 3.3 %copy-start = (bf16[2,2048,256]{2,1,0:T(8,128)(2,1)S(1)}, bf16[2,2048,256]{2,1,0:T(8,128)(2,1)}, u32[]{:S(2)}) copy-start(bf16[2,2048,256]{2,1,0:T(8,128)(2,1)} %get-tuple-element.19) | copy-start | bytes 6291460

commit v4 on v3

--- a/solution.py
+++ b/solution.py
@@ -438,6 +438,8 @@
                 b = slice(0, k * W)
                 c = slice(k * W, (k + 1) * W)
                 y = y - dot3((yh[g, :, b], yl[g, :, b]), (chi[c, b], clo[c, b]), NT)
+            if g == 1:
+                relay(0, nb - 1 - k)
             y = split(y)
             yh[g, :, k * W:(k + 1) * W] = y[0]
             yl[g, :, k * W:(k + 1) * W] = y[1]
@@ -466,9 +468,8 @@
                 home(g, k, 0, frm[0]).start()
 
             order.append((g, k))
-            if len(order) > 1:
-                relay(*order[-2])
-    relay(*order[-1])
+    for k in reversed(range(nb)):
+        relay(1, k)
     for x in sends[1]:
         x.wait_send()
     for g, k in order:

time: 283 us -> 268 us (0.947)
  Pallas kernels: 270 us -> 255 us
    pallas_call x1, Pallas kernels: 82.4 us -> 66.9 us  [exchange_call(): pl.pallas_call(functools.partial(exchange_kernel, layers), out_shape=(jax...]
where the time goes in v4:
time: 268 us; the launch traced here: 263 us
  Pallas kernels  255 us (95%)
  local copies, waits for them, and re-layouts  6.87 us (3%)
    pallas_call x1, Pallas kernels, factor_call(): pl.pallas_call(functools.partial(factor_kernel, nb, extra, interleave), o...  104 us
    pallas_call x1, Pallas kernels, gather_call(): pl.pallas_call(functools.partial(gather_kernel, decay_rate, weight, math....  84.2 us
    pallas_call x1, Pallas kernels, exchange_call(): pl.pallas_call(functools.partial(exchange_kernel, layers), out_shape=(jax...  66.9 us
    unnamed x5, local copies, waits for them, and re-layouts  6.87 us

profile of v4, /device:TPU:0, one launch (start us, length us, event | category | flops | bytes accessed | tf_op | source)
XLA Modules:
  0.0 262.6 jit_solution(1532802179520720650)
XLA Ops:
  0.6 2.3 copy.8
  2.9 84.2 %gather_gram.1 = (f32[64,256,256]{2,1,0:T(8,128)}, f32[8,128]{1,0:T(8,128)}) custom-call(bf16[2048,256]{1,0:T(8,128)(2,1)} %bitcast.9, f32[1,2048,2048]{2,1,0:T(8,128)} %prev.1), custom_call_target="tpu_custom_call" | custom-call | flops 10000000000 | bytes 30000000 | tf_op jit(solution)/shard_map/gather_gram/pallas_call | solution.py:333
  87.1 103.7 %factor.1 = (bf16[2048,2048]{1,0:T(8,128)(2,1)}, bf16[2048,2048]{1,0:T(8,128)(2,1)}, bf16[8,256,256]{2,1,0:T(8,128)(2,1)}, bf16[8,256,256]{2,1,0:T(8,128)(2,1)}, bf16[8,2,256,256]{3,2,1,0:T(8,128)(2,1)}) custom-call(s32[8,56]{1,0:T(8,128)} %constant.6.clone.dst_t, s32[8,56]{1,0:T(8,128)} %constant.7.clone.li_t, s32[8,56]{1,0:T(8,128)} %constant.8.clone.rj_t, ...), custom_call_target="tpu_custom_call" | custom-call | tf_op jit(solution)/shard_map/factor/pallas_call | solution.py:162
  190.8 66.9 %exchange_solve.1 = (bf16[2,2048,256]{2,1,0:T(8,128)(2,1)}, f32[256,2048]{1,0:T(8,128)}) custom-call(bf16[8,2,256,256]{3,2,1,0:T(8,128)(2,1)} %get-tuple-element.13.s, f32[64,256,256]{2,1,0:T(8,128)} %get-tuple-element.11.a_hbm.blocks, bf16[2048,2048]{1,0:T(8,128)(2,1)} %get-tuple-element.14.chi_h, bf16[2048,2048]{1,0:T(8,128)(2,1)} %get-tuple-element.15.clo_h, ...), custom_call_target="tpu_custom_call" | custom-call | flops 12999999488 | bytes 30000000 | tf_op jit(solution)/shard_map/exchange_solve/pallas_call | solution.py:491
  257.8 0.0 copy-start
  257.8 3.3 %copy.11 = f32[1,256,2048]{2,1,0:T(8,128)} copy(f32[1,256,2048]{2,1,0:T(8,128)} %bitcast.7) | data formatting | bytes 4194304
  261.1 0.0 copy-done
  261.1 1.3 copy.12
Async XLA Ops:
  257.8 3.3 %copy-start = (bf16[2,2048,256]{2,1,0:T(8,128)(2,1)S(1)}, bf16[2,2048,256]{2,1,0:T(8,128)(2,1)}, u32[]{:S(2)}) copy-start(bf16[2,2048,256]{2,1,0:T(8,128)(2,1)} %get-tuple-element.19) | copy-start | bytes 6291460

commit v5 on v4

--- a/solution.py
+++ b/solution.py
@@ -74,8 +74,8 @@
         assert t<=slots
     return dst,li,rj
 
-def factor_kernel(nb, extra, interleave, dst_t, li_t, rj_t, a_hbm, g_hbm, shift, chi_hbm, clo_hbm, phi_o, plo_o, s_o,
-                  blk, gst, chi, clo, uh, ul, ch, cl, half, asem, gsem, osem):
+def factor_kernel(nb, extra, sharded, dst_t, li_t, rj_t, a_hbm, g_hbm, shift, chi_hbm, clo_hbm, phi_o, plo_o, s_o, rows_o,
+                  rows_v, blk, gst, chi, clo, uh, ul, ch, cl, half, asem, gsem, osem):
     nr=nb+extra
     cslots=nr-2
     first=[]; rest=[]
@@ -92,6 +92,13 @@
         d=dst_t[k,t]; i=li_t[k,t]; j=rj_t[k,t]
         blk[d]=blk[d]-dot3((ch[i],cl[i]),(uh[j],ul[j]),NT)
 
+    orow=pltpu.make_async_copy(rows_v,rows_o,osem.at[2])
+    def own_rows():
+        dp=lax.axis_index("dp") if sharded else 3
+        for j in range(nb):
+            v=blk[jnp.maximum(dp,j)*nb+jnp.minimum(dp,j)]
+            rows_v[:,j*W:(j+1)*W]=jnp.where(jnp.full((W,W),dp,jnp.int32)>=j,v,v.T)
+
     def panel(i,k):
         u=split(blk[i*nb+k])
         uh[i]=u[0]; ul[i]=u[1]
@@ -104,9 +111,9 @@
         kk=k*nb+k
         kp=jnp.maximum(k-1,0)
         def slot(h,s):
-            if not interleave: return
-            if h==0 and s<cslots: panel(jnp.minimum(k+1+s,nr-1),kp)
-            else: tile(k,h*32+s-cslots)
+            if h==0 and s<2*cslots:
+                if s%2==0: panel(jnp.minimum(k+1+s//2,nr-1),kp)
+            else: tile(k,h*32+s-2*cslots)
         p1=sweep(blk[kk,:128,:128]+eye,lambda s: slot(0,s))
         half[0]=p1
         @pl.when(k==0)
@@ -115,6 +122,7 @@
             for j in range(nb):
                 for e in range(extra):
                     blk[(nb+e)*nb+j]=gst[e*W:(e+1)*W,j*W:(j+1)*W].astype(f32)
+            own_rows()
         d21=split(blk[kk,128:,:128])
         w=dot3(d21,split(half[0]),NN)
         sw=split(w)
@@ -127,13 +135,6 @@
         bot=jnp.concatenate([x21,p2v],axis=1)
         P=split(jnp.concatenate([top,bot],axis=0))
         phi_o[k]=P[0]; plo_o[k]=P[1]
-        if not interleave:
-            def lp(t,_):
-                tile(k,t); return 0
-            lax.fori_loop(0,jnp.where(k==0,0,jnp.int32(64)),lp,0)
-            def lc(i,_):
-                panel(i,k); return 0
-            lax.fori_loop(k+2,nr,lc,0)
         panel(k+1,k)
         @pl.when(k+1<nb)
         def _():
@@ -144,6 +145,7 @@
     o1=pltpu.make_async_copy(chi.at[pl.ds(0,nb*W)],chi_hbm,osem.at[0]); o2=pltpu.make_async_copy(clo.at[pl.ds(0,nb*W)],clo_hbm,osem.at[1])
     o1.start(); o2.start()
     for i in range(nb+1,nr): panel(i,nb-1)
+    orow.start()
     er=slice(nb*W,nr*W)
     for k in reversed(range(nb)):
         sl=slice(k*W,(k+1)*W)
@@ -154,18 +156,18 @@
         x=split(z)
         chi[er,sl]=x[0]; clo[er,sl]=x[1]
         for e in range(extra): s_o[k,e]=z[e*W:(e+1)*W].T.astype(bf)
-    o1.wait(); o2.wait()
-def factor_call(a,g,shift,interleave=True):
+    o1.wait(); o2.wait(); orow.wait()
+def factor_call(a,g,shift,sharded=True):
     n=g.shape[1]; nb=n//W; extra=g.shape[0]//W
-    t=tables(nb,extra,64-(nb+extra-2))
+    t=tables(nb,extra,64-2*(nb+extra-2))
     sm=pl.BlockSpec(memory_space=pltpu.SMEM); an=pl.BlockSpec(memory_space=pl.ANY); vm=pl.BlockSpec(memory_space=pltpu.VMEM)
     return pl.pallas_call(
-        functools.partial(factor_kernel,nb,extra,interleave),
-        out_shape=(jax.ShapeDtypeStruct((n,n),bf),jax.ShapeDtypeStruct((n,n),bf),jax.ShapeDtypeStruct((nb,W,W),bf),jax.ShapeDtypeStruct((nb,W,W),bf),jax.ShapeDtypeStruct((nb,extra,W,W),bf)),
-        in_specs=[sm,sm,sm,an,an,vm], out_specs=(an,an,vm,vm,vm),
-        scratch_shapes=[pltpu.VMEM(((nb+extra)*nb,W,W),f32),pltpu.VMEM((extra*W,n),bf),pltpu.VMEM((n+extra*W,n),bf),pltpu.VMEM((n+extra*W,n),bf),
+        functools.partial(factor_kernel,nb,extra,sharded),
+        out_shape=(jax.ShapeDtypeStruct((n,n),bf),jax.ShapeDtypeStruct((n,n),bf),jax.ShapeDtypeStruct((nb,W,W),bf),jax.ShapeDtypeStruct((nb,W,W),bf),jax.ShapeDtypeStruct((nb,extra,W,W),bf),jax.ShapeDtypeStruct((W,n),f32)),
+        in_specs=[sm,sm,sm,an,an,vm], out_specs=(an,an,vm,vm,vm,an),
+        scratch_shapes=[pltpu.VMEM((W,n),f32),pltpu.VMEM(((nb+extra)*nb,W,W),f32),pltpu.VMEM((extra*W,n),bf),pltpu.VMEM((n+extra*W,n),bf),pltpu.VMEM((n+extra*W,n),bf),
             pltpu.VMEM((nb+extra,W,W),bf),pltpu.VMEM((nb+extra,W,W),bf),pltpu.VMEM((nb+extra,W,W),bf),pltpu.VMEM((nb+extra,W,W),bf),
-            pltpu.VMEM((3,128,128),f32),pltpu.SemaphoreType.DMA((nb,nb)),pltpu.SemaphoreType.DMA((1,)),pltpu.SemaphoreType.DMA((2,))],
+            pltpu.VMEM((3,128,128),f32),pltpu.SemaphoreType.DMA((nb,nb)),pltpu.SemaphoreType.DMA((1,)),pltpu.SemaphoreType.DMA((3,))],
         compiler_params=pltpu.CompilerParams(vmem_limit_bytes=60*2**20),
         name="factor",
     )(*[jnp.asarray(x) for x in t],a,g,shift)
@@ -326,7 +328,7 @@
 def gather_call(own, prev, layers, weight):
     n, w = own.shape
     nb = n // W
-    CH = 4
+    CH = 8
     an = pl.BlockSpec(memory_space=pl.ANY)
     vm = pl.BlockSpec(memory_space=pltpu.VMEM)
     D = pltpu.SemaphoreType.DMA
@@ -343,8 +345,8 @@
     )(own, prev)
 
 
-def exchange_kernel(layers, s, blocks, chi_h, clo_h, phi_h, plo_h, out, rows_o,
-                    chi, clo, phi, plo, arr, yh, yl, xb, rl, rb, ss, sr, bs, br, rs, rr, csem, psem, rsem):
+def exchange_kernel(layers, s, chi_h, clo_h, phi_h, plo_h, out,
+                    chi, clo, phi, plo, arr, yh, yl, xb, rl, ss, sr, bs, br, rs, rr, csem, psem):
     dp = lax.axis_index("dp")
     f = lax.axis_index("factor")
     nf = lax.axis_size("factor")
@@ -382,18 +384,6 @@
             x.start()
     for x in lp:
         x.start()
-    lr = []
-    for j in range(nb):
-        idx = jnp.maximum(dp, j) * nb + jnp.minimum(dp, j)
-        x = pltpu.make_async_copy(blocks.at[idx], rb.at[j], rsem.at[j])
-        x.start()
-        lr.append(x)
-    for j in range(nb):
-        lr[j].wait()
-        v = rb[j]
-        low = jnp.full((W, W), dp, jnp.int32) >= j
-        rows_o[:, j * W:(j + 1) * W] = jnp.where(low, v, v.T)
-
     for x in sends[0]:
         x.wait_send()
     for x in sends[1]:
@@ -481,7 +471,7 @@
             onward(g, k).wait_send()
 
 
-def exchange_call(s, blocks, chi, clo, phi, plo, layers):
+def exchange_call(s, chi, clo, phi, plo, layers):
     n = chi.shape[0]
     nb = n // W
     an = pl.BlockSpec(memory_space=pl.ANY)
@@ -490,15 +480,15 @@
     V = pltpu.VMEM
     return pl.pallas_call(
         functools.partial(exchange_kernel, layers),
-        out_shape=(jax.ShapeDtypeStruct((2, n, W), bf), jax.ShapeDtypeStruct((W, n), f32)),
-        in_specs=[vm] + [an] * 5, out_specs=(an, vm),
+        out_shape=jax.ShapeDtypeStruct((2, n, W), bf),
+        in_specs=[vm] + [an] * 4, out_specs=an,
         scratch_shapes=[V((n, n), bf), V((n, n), bf), V((nb, W, W), bf), V((nb, W, W), bf), V((nb, 2, W, W), bf),
-                        V((2, W, n), bf), V((2, W, n), bf), V((2, nb, 2, W, W // 2), bf), V((2, nb, W, W // 2), bf), V((nb, W, W), f32),
-                        D((2, 8, 2)), D((2, 8, 2)), D((2, nb, 2)), D((2, nb, 2)), D((2, nb)), D((2, nb)), D((nb, 2)), D((2,)), D((nb,))],
+                        V((2, W, n), bf), V((2, W, n), bf), V((2, nb, 2, W, W // 2), bf), V((2, nb, W, W // 2), bf),
+                        D((2, 8, 2)), D((2, 8, 2)), D((2, nb, 2)), D((2, nb, 2)), D((2, nb)), D((2, nb)), D((nb, 2)), D((2,))],
         compiler_params=pltpu.CompilerParams(vmem_limit_bytes=56 * 2**20, collective_id=1, has_side_effects=True),
         cost_estimate=pl.CostEstimate(flops=13 * 10**9, bytes_accessed=3 * 10**7, transcendentals=0),
         name="exchange_solve",
-    )(s, blocks, chi, clo, phi, plo)
+    )(s, chi, clo, phi, plo)
 
 
 def per_device(features, previous, gradient):
@@ -509,8 +499,8 @@
     blocks, shift = gather_call(features[:, 0, :].T, previous, layers, weight)
     tile_rows = gradient.shape[2]
     flat = gradient[0].reshape(2 * tile_rows, block_size)
-    chi, clo, phi, plo, section_one = factor_call(blocks, flat, shift)
-    result, own_rows = exchange_call(section_one, blocks, chi, clo, phi, plo, layers)
+    chi, clo, phi, plo, section_one, own_rows = factor_call(blocks, flat, shift)
+    result = exchange_call(section_one, chi, clo, phi, plo, layers)
     return (own_rows[None], result[None])
 
 

time: 268 us -> 265 us (0.989)
  the two profiles are of different devices: /device:TPU:0 before, /device:TPU:24 now
where the time goes in v5:
time: 265 us; the launch traced here: 260 us
  Pallas kernels  254 us (96%)
  local copies, waits for them, and re-layouts  5.31 us (2%)
    pallas_call x1, Pallas kernels, factor_call(): pl.pallas_call(functools.partial(factor_kernel, nb, extra, sharded), out_...  103 us
    pallas_call x1, Pallas kernels, gather_call(): pl.pallas_call(functools.partial(gather_kernel, decay_rate, weight, math....  83.6 us
    pallas_call x1, Pallas kernels, exchange_call(): pl.pallas_call(functools.partial(exchange_kernel, layers), out_shape=jax....  67 us
    unnamed x2, local copies, waits for them, and re-layouts  5.31 us

profile of v5, /device:TPU:24, one launch (start us, length us, event | category | flops | bytes accessed | tf_op | source)
XLA Modules:
  0.0 260.1 jit_solution(2302318574828759469)
XLA Ops:
  0.6 2.3 copy.8
  2.9 83.6 %gather_gram.1 = (f32[64,256,256]{2,1,0:T(8,128)}, f32[8,128]{1,0:T(8,128)}) custom-call(bf16[2048,256]{1,0:T(8,128)(2,1)} %bitcast.8, f32[1,2048,2048]{2,1,0:T(8,128)} %prev.1), custom_call_target="tpu_custom_call" | custom-call | flops 10000000000 | bytes 30000000 | tf_op jit(solution)/shard_map/gather_gram/pallas_call | solution.py:335
  86.5 103.4 %factor.1 = (bf16[2048,2048]{1,0:T(8,128)(2,1)}, bf16[2048,2048]{1,0:T(8,128)(2,1)}, bf16[8,256,256]{2,1,0:T(8,128)(2,1)}, bf16[8,256,256]{2,1,0:T(8,128)(2,1)},...) custom-call(s32[8,48]{1,0:T(8,128)} %constant.6.clone.dst_t, s32[8,48]{1,0:T(8,128)} %constant.7.clone.li_t, ...), custom_call_target="tpu_custom_call" | custom-call | tf_op jit(solution)/shard_map/factor/pallas_call | solution.py:164
  189.9 67.0 %exchange_solve.1 = bf16[2,2048,256]{2,1,0:T(8,128)(2,1)} custom-call(bf16[8,2,256,256]{3,2,1,0:T(8,128)(2,1)} %get-tuple-element.13.s, bf16[2048,2048]{1,0:T(8,128)(2,1)} %get-tuple-element.14.chi_h, bf16[2048,2048]{1,0:T(8,128)(2,1)} %get-tuple-element.15.clo_h, bf16[8,256,256]{2,1,0:T(8,128)(2,1)} %get-tuple-element.16.phi_h, ...), custom_call_target="tpu_custom_call" | custom-call | flops 12999999488 | bytes 30000000 | tf_op jit(solution)/shard_map/exchange_solve/pallas_call | solution.py:481
  256.9 3.0 %copy.10 = bf16[1,2,2048,256]{3,2,1,0:T(8,128)(2,1)} copy(bf16[1,2,2048,256]{3,2,1,0:T(8,128)(2,1)} %bitcast.6) | data formatting | bytes 4194304
